TPU v7x, 32 devices: a whole 2x2x4 slice. The times are simulated.
32 devices in a mesh: dp: 2 (over x), row: 4 (over z), col: 4 (over y, core).
Axes of the slice: x: 2, y: 2, z: 4, core: 2. Of those that a mesh axis runs over, the one named last changes fastest.
Arguments:
- block_in: bfloat16 [4096, 1088], P(('dp', 'col'), 'row'), may hold values from -6 to 6
- cotangent: bfloat16 [4096, 1088], P(('dp', 'col'), 'row'), may hold values from -0.0390625 to 0.0390625
- lengths: int32 [8, 3], P(('dp', 'row')), may hold values from 1 to 384, 512 in all within a row
- qkv_weight: float32 [1088, 4, 816], P('row', 'col', 'dp'), may hold values from -0.1875 to 0.1875
- proj_weight: float32 [1088, 4, 272], P('col', 'row', 'dp'), may hold values from -1.5 to 1.5
- fc1_weight: float32 [1088, 4, 1088], P('row', 'col', 'dp'), may hold values from -0.25 to 0.25
- fc2_weight: float32 [4352, 4, 272], P('col', 'row', 'dp'), may hold values from -0.1875 to 0.1875
- qkv_bias: float32 [4, 816], P('col', 'dp'), may hold values from -1.5 to 1.5
- fc1_bias: float32 [4, 1088], P('col', 'dp'), may hold values from -1.75 to 1.75
- row_vectors: float32 [6, 4, 272], P(None, 'row', 'dp'), may hold values from -1.5 to 1.5, as said below
- qkv_moments: float32 [2, 1088, 4, 816], P(None, 'row', 'col', 'dp'), may hold values from -0.45 to 0.45, as said below
- proj_moments: float32 [2, 1088, 4, 272], P(None, 'col', 'row', 'dp'), may hold values from -0.075 to 0.075, as said below
- fc1_moments: float32 [2, 1088, 4, 1088], P(None, 'row', 'col', 'dp'), may hold values from -0.105 to 0.105, as said below
- fc2_moments: float32 [2, 4352, 4, 272], P(None, 'col', 'row', 'dp'), may hold values from -0.18 to 0.18, as said below
- qkv_bias_moments: float32 [2, 4, 816], P(None, 'col', 'dp'), may hold values from -0.75 to 0.75, as said below
- fc1_bias_moments: float32 [2, 4, 1088], P(None, 'col', 'dp'), may hold values from -0.105 to 0.105, as said below
- row_moments: float32 [2, 6, 4, 272], P(None, None, 'row', 'dp'), may hold values from -0.6 to 0.6, as said below
Outputs:
- block_out: bfloat16 [4096, 1088], P(('dp', 'col'), 'row')
- block_in_grad: float32 [4096, 1088], P(('dp', 'col'), 'row')
- qkv_weight_grad: float32 [1088, 4, 816], P('row', 'col', 'dp')
- proj_weight_grad: float32 [1088, 4, 272], P('col', 'row', 'dp')
- fc1_weight_grad: float32 [1088, 4, 1088], P('row', 'col', 'dp')
- fc2_weight_grad: float32 [4352, 4, 272], P('col', 'row', 'dp')
- qkv_bias_grad: float32 [4, 816], P('col', 'dp')
- fc1_bias_grad: float32 [4, 1088], P('col', 'dp')
- row_vectors_grad: float32 [6, 4, 272], P(None, 'row', 'dp')
- qkv_weight_new: float32 [1088, 4, 816], P('row', 'col', 'dp')
- proj_weight_new: float32 [1088, 4, 272], P('col', 'row', 'dp')
- fc1_weight_new: float32 [1088, 4, 1088], P('row', 'col', 'dp')
- fc2_weight_new: float32 [4352, 4, 272], P('col', 'row', 'dp')
- qkv_bias_new: float32 [4, 816], P('col', 'dp')
- fc1_bias_new: float32 [4, 1088], P('col', 'dp')
- row_vectors_new: float32 [6, 4, 272], P(None, 'row', 'dp')
- qkv_moments_new: float32 [2, 1088, 4, 816], P(None, 'row', 'col', 'dp')
- proj_moments_new: float32 [2, 1088, 4, 272], P(None, 'col', 'row', 'dp')
- fc1_moments_new: float32 [2, 1088, 4, 1088], P(None, 'row', 'col', 'dp')
- fc2_moments_new: float32 [2, 4352, 4, 272], P(None, 'col', 'row', 'dp')
- qkv_bias_moments_new: float32 [2, 4, 816], P(None, 'col', 'dp')
- fc1_bias_moments_new: float32 [2, 4, 1088], P(None, 'col', 'dp')
- row_moments_new: float32 [2, 6, 4, 272], P(None, None, 'row', 'dp')
Inputs may be any that keep to these rules, and one draw needn't show every extreme that they name: In every row the 3 lengths sum to 512 and one of them equals 384. `row_vectors`: rows 0 and 3 are gains, the other rows biases. `qkv_moments`: index 0 holds first moments, index 1 second moments, which are positive. `proj_moments`: index 0 holds first moments, index 1 second moments, which are positive. `fc1_moments`: index 0 holds first moments, index 1 second moments, which are positive. `fc2_moments`: index 0 holds first moments, index 1 second moments, which are positive. `qkv_bias_moments`: index 0 holds first moments, index 1 second moments, which are positive. `fc1_bias_moments`: index 0 holds first moments, index 1 second moments, which are positive. `row_moments`: index 0 holds first moments, index 1 second moments, which are positive.
All inputs are finite; a program needn't handle non-finite values.
Results may differ from a plain program's by a relative error of at most 0.018.
Values may be sent and summed in bfloat16 or wider, within the bound.
A program may use at most 128 MiB of HBM per device.

v0:
```python
import jax
import jax.numpy as jnp
from jax import lax
from jax.sharding import PartitionSpec as P

D = 1088
H = 17
HD = 64
STEP = 3


NORM_EPS = 1e-05
BETA_ONE = 0.9
BETA_TWO = 0.95
LEARN_RATE = 0.05
VECTOR_RATE = 0.2
DECAY_RATE = 0.1
ADAM_EPS = 1e-08


def gelu_tanh(values_in):
    return jax.nn.gelu(values_in, approximate=True)


def weigh(row_block, weight, transposed):
    return lax.dot_general(
        row_block,
        weight,
        (((1,), (1 if transposed else 0,)), ((), ())),
        preferred_element_type=jnp.float32,
    )


def outer_sum(left_rows, right_rows):
    return lax.dot_general(
        left_rows, right_rows, (((0,), (0,)), ((), ())), preferred_element_type=jnp.float32
    )


def gather_cols(tokens_block):
    return lax.all_gather(tokens_block, "col", axis=0, tiled=True)


def gather_rows(tokens_block):
    return lax.all_gather(tokens_block, "row", axis=0, tiled=True)


def across_rows(gathered, weight, transposed):
    share_rows = gathered.shape[0] // lax.axis_size("row")

    def partial_term(row_start, row_count):
        return weigh(gathered, weight, transposed)

    return lax.psum_scatter(
        partial_term(jnp.int32(0), share_rows * lax.axis_size("row")),
        "row",
        scatter_dimension=0,
        tiled=True,
    )


def across_cols(gathered, weight, transposed):
    share_rows = gathered.shape[0] // lax.axis_size("col")

    def partial_term(row_start, row_count):
        return weigh(gathered, weight, transposed)

    return lax.psum_scatter(
        partial_term(jnp.int32(0), share_rows * lax.axis_size("col")),
        "col",
        scatter_dimension=0,
        tiled=True,
    )


def feature_sums(first_sum, second_sum):
    return lax.psum((first_sum, second_sum), "row")


def norm_forward(values_in, gain_row, shift_row):
    row_total, row_squares = feature_sums(
        jnp.sum(values_in, axis=1), jnp.sum(values_in * values_in, axis=1)
    )
    row_mean = row_total[:, None] / D
    spread = row_squares[:, None] / D - row_mean * row_mean
    inv_scale = lax.rsqrt(spread + NORM_EPS)
    centred = (values_in - row_mean) * inv_scale
    return ((centred * gain_row + shift_row).astype(jnp.bfloat16), centred, inv_scale)


def norm_backward(upstream, centred, inv_scale, gain_row):
    pushed = upstream * gain_row
    row_total, cross_sum = feature_sums(jnp.sum(pushed, axis=1), jnp.sum(pushed * centred, axis=1))
    result = inv_scale * (pushed - row_total[:, None] / D - centred * (cross_sum[:, None] / D))
    return (result, jnp.sum(upstream * centred, axis=0), jnp.sum(upstream, axis=0))


def attention_scores(queries, key_heads, allowed):
    scores = jnp.einsum(
        "qhd,khd->hqk", queries, key_heads, preferred_element_type=jnp.float32
    ) * HD ** (-0.5)
    return jnp.where(allowed[None], scores, -1e30)


def adam_step(master, moment, gradient, decay_rate, step_rate):
    first_moment = BETA_ONE * moment[0] + (1.0 - BETA_ONE) * gradient
    second_moment = BETA_TWO * moment[1] + (1.0 - BETA_TWO) * gradient * gradient
    change = (
        first_moment
        / (1.0 - BETA_ONE**STEP)
        / (jnp.sqrt(second_moment / (1.0 - BETA_TWO**STEP)) + ADAM_EPS)
    )
    change = change + decay_rate * master
    return (master - step_rate * change, jnp.stack([first_moment, second_moment]))


def on_device(
    block_in,
    cotangent,
    lengths,
    qkv_weight,
    proj_weight,
    fc1_weight,
    fc2_weight,
    qkv_bias,
    fc1_bias,
    row_vectors,
    qkv_moments,
    proj_moments,
    fc1_moments,
    fc2_moments,
    qkv_bias_moments,
    fc1_bias_moments,
    row_moments,
):
    wide_type = jnp.float32
    short_type = jnp.bfloat16
    copies = (
        lax.all_gather(qkv_weight.astype(short_type), "dp", axis=2, tiled=True),
        lax.all_gather(proj_weight.astype(short_type), "dp", axis=2, tiled=True),
        lax.all_gather(fc1_weight.astype(short_type), "dp", axis=2, tiled=True),
        lax.all_gather(fc2_weight.astype(short_type), "dp", axis=2, tiled=True),
        lax.all_gather(qkv_bias.astype(short_type)[:, None, :], "dp", axis=2, tiled=True),
        lax.all_gather(fc1_bias.astype(short_type)[:, None, :], "dp", axis=2, tiled=True),
        lax.all_gather(row_vectors.astype(short_type), "dp", axis=2, tiled=True),
    )
    w_qkv = copies[0][:, 0, :]
    w_proj = copies[1][:, 0, :]
    w_fc1 = copies[2][:, 0, :]
    w_fc2 = copies[3][:, 0, :]
    bias_qkv = copies[4][0, 0, :].astype(wide_type)
    bias_fc1 = copies[5][0, 0, :].astype(wide_type)
    vectors = copies[6][:, 0, :].astype(wide_type)
    x_full = block_in.astype(wide_type)
    normed_one, centred_one, scale_one = norm_forward(x_full, vectors[0], vectors[1])
    inputs_one = gather_cols(normed_one)
    mixed_qkv = (across_rows(inputs_one, w_qkv, False) + bias_qkv).astype(short_type)
    whole_qkv = lax.all_gather(mixed_qkv, "col", axis=1, tiled=True)
    pack_len = whole_qkv.shape[0]
    query_rows = pack_len // lax.axis_size("col")
    query_start = lax.axis_index("col") * query_rows
    seq_ends = jnp.cumsum(lengths[0])
    places = jnp.arange(pack_len, dtype=jnp.int32)
    segment = jnp.sum((places[:, None] >= seq_ends[None, :]).astype(jnp.int32), axis=1)
    query_places = query_start + jnp.arange(query_rows, dtype=jnp.int32)
    query_segment = lax.dynamic_slice_in_dim(segment, query_start, query_rows, 0)
    allowed = (query_segment[:, None] == segment[None, :]) & (
        places[None, :] <= query_places[:, None]
    )
    queries = lax.dynamic_slice_in_dim(whole_qkv, query_start, query_rows, 0)[:, :D].reshape(
        query_rows, H, HD
    )
    key_heads = whole_qkv[:, D : 2 * D].reshape(pack_len, H, HD)
    value_heads = whole_qkv[:, 2 * D :].reshape(pack_len, H, HD)
    scores = attention_scores(queries, key_heads, allowed)
    row_top = jnp.max(scores, axis=2, keepdims=True)
    log_total = row_top + jnp.log(jnp.sum(jnp.exp(scores - row_top), axis=2, keepdims=True))
    weights = jnp.exp(scores - log_total).astype(short_type)
    attended = (
        jnp.einsum("hqk,khd->qhd", weights, value_heads, preferred_element_type=wide_type)
        .astype(short_type)
        .reshape(query_rows, D)
    )
    heads_feat = lax.all_to_all(attended, "col", split_axis=1, concat_axis=0, tiled=True)
    inputs_att = gather_rows(heads_feat)
    x_mid = x_full + across_cols(inputs_att, w_proj, False) + vectors[2]
    normed_two, centred_two, scale_two = norm_forward(x_mid, vectors[3], vectors[4])
    inputs_two = gather_cols(normed_two)
    pre_act = across_rows(inputs_two, w_fc1, False) + bias_fc1
    hidden = gelu_tanh(pre_act).astype(short_type)
    inputs_hid = gather_rows(hidden)
    block_out = (x_mid + across_cols(inputs_hid, w_fc2, False) + vectors[5]).astype(short_type)
    grad_out = gather_cols(cotangent)
    grad_hidden = across_rows(grad_out, w_fc2, True)
    grad_fc2 = outer_sum(inputs_hid, grad_out)
    grad_bias_two = jnp.sum(grad_out, axis=0, dtype=wide_type)
    pullback = jax.vjp(gelu_tanh, pre_act)[1]
    grad_pre = pullback(grad_hidden)[0].astype(short_type)
    pre_rows = gather_rows(grad_pre)
    grad_normed_two = across_cols(pre_rows, w_fc1, True)
    grad_fc1 = outer_sum(inputs_two, pre_rows)
    grad_bias_fc1 = jnp.sum(pre_rows, axis=0, dtype=wide_type)
    back_two, grad_gain_two, grad_shift_two = norm_backward(
        grad_normed_two, centred_two, scale_two, vectors[3]
    )
    grad_mid = cotangent.astype(wide_type) + back_two
    mid_cols = gather_cols(grad_mid.astype(short_type))
    grad_heads = across_rows(mid_cols, w_proj, True).astype(short_type)
    grad_proj = outer_sum(inputs_att, mid_cols)
    grad_bias_proj = jnp.sum(mid_cols, axis=0, dtype=wide_type)
    grad_attended = lax.all_to_all(
        grad_heads, "col", split_axis=0, concat_axis=1, tiled=True
    ).reshape(query_rows, H, HD)
    probs_full = jnp.exp(attention_scores(queries, key_heads, allowed) - log_total)
    grad_values = jnp.einsum(
        "hqk,qhd->khd", weights, grad_attended, preferred_element_type=wide_type
    )
    grad_probs = jnp.einsum(
        "qhd,khd->hqk", grad_attended, value_heads, preferred_element_type=wide_type
    )
    row_delta = jnp.sum(
        grad_attended.astype(wide_type) * attended.reshape(query_rows, H, HD).astype(wide_type),
        axis=2,
    )
    grad_scores = (probs_full * (grad_probs - row_delta.T[:, :, None]) * HD ** (-0.5)).astype(
        short_type
    )
    grad_query = jnp.einsum(
        "hqk,khd->qhd", grad_scores, key_heads, preferred_element_type=wide_type
    ).reshape(query_rows, D)
    grad_keys = jnp.einsum(
        "hqk,qhd->khd", grad_scores, queries, preferred_element_type=wide_type
    ).reshape(pack_len, D)
    placed = lax.dynamic_update_slice_in_dim(
        jnp.zeros((pack_len, D), wide_type), grad_query, query_start, 0
    )
    grad_whole = jnp.concatenate([placed, grad_keys, grad_values.reshape(pack_len, D)], axis=1)
    grad_mixed = (
        lax.psum_scatter(grad_whole.astype(jnp.bfloat16), "col", scatter_dimension=1, tiled=True)
        .astype(jnp.float32)
        .astype(short_type)
    )
    mixed_rows = gather_rows(grad_mixed)
    grad_normed_one = across_cols(mixed_rows, w_qkv, True)
    grad_qkv = outer_sum(inputs_one, mixed_rows)
    grad_bias_qkv = jnp.sum(mixed_rows, axis=0, dtype=wide_type)
    back_one, grad_gain_one, grad_shift_one = norm_backward(
        grad_normed_one, centred_one, scale_one, vectors[0]
    )
    block_in_grad = grad_mid + back_one
    norm_grads = lax.psum((grad_gain_one, grad_shift_one, grad_gain_two, grad_shift_two), "col")
    row_grads = jnp.stack(
        [norm_grads[0], norm_grads[1], grad_bias_proj, norm_grads[2], norm_grads[3], grad_bias_two]
    )[:, None, :]
    shards = (
        lax.psum_scatter(
            grad_qkv[:, None, :].astype(jnp.bfloat16), "dp", scatter_dimension=2, tiled=True
        ).astype(jnp.float32),
        lax.psum_scatter(
            grad_proj[:, None, :].astype(jnp.bfloat16), "dp", scatter_dimension=2, tiled=True
        ).astype(jnp.float32),
        lax.psum_scatter(
            grad_fc1[:, None, :].astype(jnp.bfloat16), "dp", scatter_dimension=2, tiled=True
        ).astype(jnp.float32),
        lax.psum_scatter(
            grad_fc2[:, None, :].astype(jnp.bfloat16), "dp", scatter_dimension=2, tiled=True
        ).astype(jnp.float32),
        lax.psum_scatter(
            grad_bias_qkv[None, None, :].astype(jnp.bfloat16), "dp", scatter_dimension=2, tiled=True
        ).astype(jnp.float32),
        lax.psum_scatter(
            grad_bias_fc1[None, None, :].astype(jnp.bfloat16), "dp", scatter_dimension=2, tiled=True
        ).astype(jnp.float32),
        lax.psum_scatter(
            row_grads.astype(jnp.bfloat16), "dp", scatter_dimension=2, tiled=True
        ).astype(jnp.float32),
    )
    grads = (shards[0], shards[1], shards[2], shards[3], shards[4][0], shards[5][0], shards[6])
    masters = (qkv_weight, proj_weight, fc1_weight, fc2_weight, qkv_bias, fc1_bias, row_vectors)
    moments = (
        qkv_moments,
        proj_moments,
        fc1_moments,
        fc2_moments,
        qkv_bias_moments,
        fc1_bias_moments,
        row_moments,
    )
    decays = (DECAY_RATE, DECAY_RATE, DECAY_RATE, DECAY_RATE, 0.0, 0.0, 0.0)
    rates = (LEARN_RATE, LEARN_RATE, LEARN_RATE, LEARN_RATE, VECTOR_RATE, VECTOR_RATE, VECTOR_RATE)
    updates = [
        adam_step(master, moment, gradient, decay_rate, step_rate)
        for master, moment, gradient, decay_rate, step_rate in zip(
            masters, moments, grads, decays, rates
        )
    ]
    return (
        block_out,
        block_in_grad,
        grads[0],
        grads[1],
        grads[2],
        grads[3],
        grads[4],
        grads[5],
        grads[6],
        updates[0][0],
        updates[1][0],
        updates[2][0],
        updates[3][0],
        updates[4][0],
        updates[5][0],
        updates[6][0],
        updates[0][1],
        updates[1][1],
        updates[2][1],
        updates[3][1],
        updates[4][1],
        updates[5][1],
        updates[6][1],
    )


def solution(mesh):
    in_specs = (
        P(("dp", "col"), "row"),
        P(("dp", "col"), "row"),
        P(("dp", "row"), None),
        P("row", "col", "dp"),
        P("col", "row", "dp"),
        P("row", "col", "dp"),
        P("col", "row", "dp"),
        P("col", "dp"),
        P("col", "dp"),
        P(None, "row", "dp"),
        P(None, "row", "col", "dp"),
        P(None, "col", "row", "dp"),
        P(None, "row", "col", "dp"),
        P(None, "col", "row", "dp"),
        P(None, "col", "dp"),
        P(None, "col", "dp"),
        P(None, None, "row", "dp"),
    )
    out_specs = (
        P(("dp", "col"), "row"),
        P(("dp", "col"), "row"),
        P("row", "col", "dp"),
        P("col", "row", "dp"),
        P("row", "col", "dp"),
        P("col", "row", "dp"),
        P("col", "dp"),
        P("col", "dp"),
        P(None, "row", "dp"),
        P("row", "col", "dp"),
        P("col", "row", "dp"),
        P("row", "col", "dp"),
        P("col", "row", "dp"),
        P("col", "dp"),
        P("col", "dp"),
        P(None, "row", "dp"),
        P(None, "row", "col", "dp"),
        P(None, "col", "row", "dp"),
        P(None, "row", "col", "dp"),
        P(None, "col", "row", "dp"),
        P(None, "col", "dp"),
        P(None, "col", "dp"),
        P(None, None, "row", "dp"),
    )
    return jax.shard_map(
        on_device, mesh=mesh, in_specs=in_specs, out_specs=out_specs, check_vma=False
    )
```

profile of v0, /device:TPU:0, one launch (start us, length us, event | category | flops | bytes accessed | tf_op | source)
XLA Modules:
  0.0 1226.2 jit_solution(12979779135581023099)
XLA Ops:
  8.1 5.9 all_gather.48
  14.2 6.3 slice_reduce_fusion
  21.5 12.5 %all-reduce.11 = (f32[512]{0:T(512)S(1)}, f32[512]{0:T(512)S(1)}) all-reduce(f32[512]{0:T(512)S(1)} %get-tuple-element.172, f32[512]{0:T(512)S(1)} %get-tuple-element.171), channel_id=1, replica_groups=mesh['dp'=2,'row'=4,'col'=4] {'row'}, use_global_device_ids=true, to_apply=%region_3.0 | all-reduce | flops 1024 | bytes 8192 | tf_op jit(solution)/shard_map/psum | solution.py:77
  37.0 13.4 %all_gather.50 = bf16[272,1,816]{0,1,2:T(2,128)(2,1)S(1)} all-gather(bf16[272,1,408]{0,1,2:T(2,128)(2,1)S(1)} %copy.170), channel_id=1, replica_groups=mesh['dp'=2,'row'=4,'col'=4] {'dp'}, dimensions={2}, use_global_device_ids=true | all-gather | bytes 665856 | tf_op jit(solution)/shard_map/all_gather | solution.py:139
  54.0 6.1 fusion.46
  68.8 106.9 %reduce-scatter.24.cloned.1.call-done = f32[512,816]{0,1:T(8,128)} async-done(((f32[2048,816]{0,1:T(8,128)}), f32[512,816]{0,1:T(8,128)}) %reduce-scatter.24.cloned.1.call-update) | async-done | bytes 1671184 | tf_op jit(solution)/shard_map/reduce_scatter | solution.py:54
  179.0 29.5 %all-gather.14.cloned.1.call-done = bf16[512,3264]{0,1:T(8,128)(2,1)} async-done(((bf16[512,816]{0,1:T(8,128)(2,1)}), bf16[512,3264]{0,1:T(8,128)(2,1)}) %all-gather.14.cloned.1.call-update) | async-done | bytes 3342352 | tf_op jit(solution)/shard_map/all_gather | solution.py:158
  215.8 8.6 all_to_all.35
  230.7 23.5 %all-gather.16.cloned.1.call-done = bf16[2048,272]{0,1:T(8,128)(2,1)} async-done(((bf16[512,272]{0,1:T(8,128)(2,1)}), bf16[2048,272]{0,1:T(8,128)(2,1)}) %all-gather.16.cloned.1.call-update) | async-done | bytes 1114128 | tf_op jit(solution)/shard_map/all_gather | solution.py:45
  258.3 31.2 %reduce-scatter.26.cloned.1.call-done = f32[512,272]{0,1:T(8,128)} async-done(((f32[2048,272]{0,1:T(8,128)}), f32[512,272]{0,1:T(8,128)}) %reduce-scatter.26.cloned.1.call-update) | async-done | bytes 557072 | tf_op jit(solution)/shard_map/reduce_scatter | solution.py:68
  290.8 11.7 all-reduce.10
  303.5 7.8 all_gather.59
  311.3 7.5 fusion.18
  323.0 18.2 %all_gather.56 = bf16[272,1,1088]{0,1,2:T(2,128)(2,1)} all-gather(bf16[272,1,544]{0,1,2:T(2,128)(2,1)S(1)} %copy.174), channel_id=1, replica_groups=mesh['dp'=2,'row'=4,'col'=4] {'dp'}, dimensions={2}, use_global_device_ids=true | all-gather | bytes 887808 | tf_op jit(solution)/shard_map/all_gather | solution.py:141
  345.7 7.2 fusion.24
  353.6 129.2 %reduce-scatter.32.cloned.1.call-done = f32[512,1088]{0,1:T(8,128)} async-done(((f32[2048,1088]{0,1:T(8,128)}), f32[512,1088]{0,1:T(8,128)}) %reduce-scatter.32.cloned.1.call-update) | async-done | bytes 2228240 | tf_op jit(solution)/shard_map/reduce_scatter | solution.py:54
  482.8 156.2 %reduce-scatter.28.cloned.1.call-done = f32[512,1088]{0,1:T(8,128)} async-done(((f32[2048,1088]{0,1:T(8,128)}), f32[512,1088]{0,1:T(8,128)}) %reduce-scatter.28.cloned.1.call-update) | async-done | bytes 2228240 | tf_op jit(solution)/shard_map/reduce_scatter | solution.py:54
  643.5 12.6 %reduce-scatter.34.cloned.1.call-start = ((), (), s32[]{:S(2)}) async-start(), calls=%async_computation.26 | async-start | bytes 2785280 | tf_op jit(solution)/shard_map/reduce_scatter | solution.py:68
  656.1 73.5 %all-gather.24.cloned.1.call-done = bf16[2048,1088]{0,1:T(8,128)(2,1)} async-done(((bf16[512,1088]{0,1:T(8,128)(2,1)}), bf16[2048,1088]{0,1:T(8,128)(2,1)}) %all-gather.24.cloned.1.call-update) | async-done | bytes 4456464 | tf_op jit(solution)/shard_map/all_gather | solution.py:45
  735.0 30.8 %reduce-scatter.34.cloned.1.call-done = f32[512,272]{0,1:T(8,128)} async-done(((f32[2048,272]{0,1:T(8,128)}), f32[512,272]{0,1:T(8,128)}) %reduce-scatter.34.cloned.1.call-update) | async-done | bytes 557072 | tf_op jit(solution)/shard_map/reduce_scatter | solution.py:68
  767.7 11.7 all-reduce.9
  781.4 14.4 %all-gather.26.cloned.1.call-done = bf16[2048,272]{0,1:T(8,128)(2,1)} async-done(((bf16[512,272]{0,1:T(8,128)(2,1)}), bf16[2048,272]{0,1:T(8,128)(2,1)}) %all-gather.26.cloned.1.call-update) | async-done | bytes 1114128 | tf_op jit(solution)/shard_map/all_gather | solution.py:41
  799.4 46.1 %reduce-scatter.36.cloned.1.call-done = f32[512,272]{0,1:T(8,128)} async-done(((f32[2048,272]{0,1:T(8,128)}), f32[512,272]{0,1:T(8,128)}) %reduce-scatter.36.cloned.1.call-update) | async-done | bytes 557072 | tf_op jit(solution)/shard_map/reduce_scatter | solution.py:54
  846.6 8.7 all_to_all.36
  866.7 37.2 %reduce-scatter.38.cloned.1.call-done = bf16[512,816]{0,1:T(8,128)(2,1)} async-done(((bf16[512,3264]{0,1:T(8,128)(2,1)}), bf16[512,816]{0,1:T(8,128)(2,1)}) %reduce-scatter.38.cloned.1.call-update) | async-done | bytes 835600 | tf_op jit(solution)/shard_map/reduce_scatter | solution.py:239
  921.0 70.2 %all-gather.20.cloned.1.call-done = bf16[2048,1088]{0,1:T(8,128)(2,1)} async-done(((bf16[512,1088]{0,1:T(8,128)(2,1)}), bf16[2048,1088]{0,1:T(8,128)(2,1)}) %all-gather.20.cloned.1.call-update) | async-done | bytes 4456464 | tf_op jit(solution)/shard_map/all_gather | solution.py:45
  999.1 58.7 %all-gather.28.cloned.1.call-done = bf16[2048,816]{0,1:T(8,128)(2,1)} async-done(((bf16[512,816]{0,1:T(8,128)(2,1)}), bf16[2048,816]{0,1:T(8,128)(2,1)}) %all-gather.28.cloned.1.call-update) | async-done | bytes 3342352 | tf_op jit(solution)/shard_map/all_gather | solution.py:45
  1100.3 10.2 reduce-scatter.46.cloned.1.call-done
  1121.0 25.4 %all-reduce.17.cloned.1.call-done = (bf16[272,1,816]{2,0,1:T(8,128)(2,1)}, bf16[272,1,272]{2,0,1:T(8,128)(2,1)}) async-done(((bf16[272,1,816]{2,0,1:T(8,128)(2,1)}, bf16[272,1,272]{2,0,1:T(8,128)(2,1)}), (bf16[272,1,816]{2,0,1:T(8,128)(2,1)}, bf16[272,1,272]{2,0,1:T(8,128)(2,1)})) %all-reduce.17.cloned.1.call-update) | async-done | bytes 591888
  1158.2 23.4 %reduce-scatter.40.cloned.1.call-done = f32[512,272]{0,1:T(8,128)} async-done(((f32[2048,272]{0,1:T(8,128)}), f32[512,272]{0,1:T(8,128)}) %reduce-scatter.40.cloned.1.call-update) | async-done | bytes 557072 | tf_op jit(solution)/shard_map/reduce_scatter | solution.py:68
  1188.9 8.3 all-reduce.12
  1197.2 11.6 all-reduce.8
  (314 shorter events, 183.5 us)
Async XLA Ops:
  7.2 46.8 %all-gather.12.cloned.1.call-start = ((), (), s32[]{:S(2)}) async-start(), calls=%async_computation.14 | async-start | bytes 1392640 | tf_op jit(solution)/shard_map/all_gather | solution.py:41
  35.9 139.8 %reduce-scatter.24.cloned.1.call-start = ((), (), s32[]{:S(2)}) async-start(), calls=%async_computation.15 | async-start | bytes 8355840 | tf_op jit(solution)/shard_map/reduce_scatter | solution.py:54
  60.2 118.3 %copy-start.70 = (s32[1,3]{1,0:T(1,128)S(1)}, s32[1,3]{1,0:T(1,128)}, u32[]{:S(2)}) copy-start(s32[1,3]{1,0:T(1,128)} %param.19) | copy-start | bytes 40
  60.2 148.3 %all-gather.14.cloned.1.call-start = ((), (), s32[]{:S(2)}) async-start(), calls=%async_computation.16 | async-start | bytes 4177920 | tf_op jit(solution)/shard_map/all_gather | solution.py:158
  178.2 76.1 %all-gather.16.cloned.1.call-start = ((), (), s32[]{:S(2)}) async-start(), calls=%async_computation.17 | async-start | bytes 1392640 | tf_op jit(solution)/shard_map/all_gather | solution.py:45
  225.1 64.4 %reduce-scatter.26.cloned.1.call-start = ((), (), s32[]{:S(2)}) async-start(), calls=%async_computation.18 | async-start | bytes 2785280 | tf_op jit(solution)/shard_map/reduce_scatter | solution.py:68
  257.7 53.6 %all-gather.22.cloned.1.call-start = ((), (), s32[]{:S(2)}) async-start(), calls=%async_computation.23 | async-start | bytes 1392640 | tf_op jit(solution)/shard_map/all_gather | solution.py:41
  258.3 87.4 %all-gather.18.cloned.1.call-start = ((), (), s32[]{:S(2)}) async-start(), calls=%async_computation.19 | async-start | bytes 1392640 | tf_op jit(solution)/shard_map/all_gather | solution.py:41
  303.4 179.4 %reduce-scatter.32.cloned.1.call-start = ((), (), s32[]{:S(2)}) async-start(), calls=%async_computation.24 | async-start | bytes 11141120 | tf_op jit(solution)/shard_map/reduce_scatter | solution.py:54
  318.8 320.2 %reduce-scatter.28.cloned.1.call-start = ((), (), s32[]{:S(2)}) async-start(), calls=%async_computation.20 | async-start | bytes 11141120 | tf_op jit(solution)/shard_map/reduce_scatter | solution.py:54
  352.9 376.7 %all-gather.24.cloned.1.call-start = ((), (), s32[]{:S(2)}) async-start(), calls=%async_computation.25 | async-start | bytes 5570560 | tf_op jit(solution)/shard_map/all_gather | solution.py:45
  643.5 122.2 %reduce-scatter.34.cloned.1.call-start = ((), (), s32[]{:S(2)}) async-start(), calls=%async_computation.26 | async-start | bytes 2785280 | tf_op jit(solution)/shard_map/reduce_scatter | solution.py:68
  734.9 60.9 %all-gather.26.cloned.1.call-start = ((), (), s32[]{:S(2)}) async-start(), calls=%async_computation.27 | async-start | bytes 1392640 | tf_op jit(solution)/shard_map/all_gather | solution.py:41
  781.3 64.1 %reduce-scatter.36.cloned.1.call-start = ((), (), s32[]{:S(2)}) async-start(), calls=%async_computation.28 | async-start | bytes 2785280 | tf_op jit(solution)/shard_map/reduce_scatter | solution.py:54
  799.3 104.6 %reduce-scatter.38.cloned.1.call-start = ((), (), s32[]{:S(2)}) async-start(), calls=%async_computation.29 | async-start | bytes 4177920 | tf_op jit(solution)/shard_map/reduce_scatter | solution.py:239
  866.1 125.0 %all-gather.20.cloned.1.call-start = ((), (), s32[]{:S(2)}) async-start(), calls=%async_computation.21 | async-start | bytes 5570560 | tf_op jit(solution)/shard_map/all_gather | solution.py:45
  866.7 191.1 %all-gather.28.cloned.1.call-start = ((), (), s32[]{:S(2)}) async-start(), calls=%async_computation.30 | async-start | bytes 4177920 | tf_op jit(solution)/shard_map/all_gather | solution.py:45
  903.9 180.6 %reduce-scatter.44.cloned.1.call-start = ((), (), s32[]{:S(2)}) async-start(), calls=%async_computation.33 | async-start | bytes 417792
  911.4 180.3 %reduce-scatter.42.cloned.1.call-start = ((), (), s32[]{:S(2)}) async-start(), calls=%async_computation.32 | async-start | bytes 1253376
  920.9 75.3 %copy-start.4 = (bf16[2048,272]{0,1:T(8,128)(2,1)S(1)}, bf16[2048,272]{0,1:T(8,128)(2,1)}, u32[]{:S(2)}) copy-start(bf16[2048,272]{0,1:T(8,128)(2,1)} %all-gather.26.cloned.1.call-done) | copy-start | bytes 3342340
  920.9 189.6 %reduce-scatter.46.cloned.1.call-start = ((), (), s32[]{:S(2)}) async-start(), calls=%async_computation.34 | async-start | bytes 940032
  996.2 61.6 %copy-start.19 = (bf16[2048,272]{0,1:T(8,128)(2,1)S(1)}, bf16[2048,272]{0,1:T(8,128)(2,1)}, u32[]{:S(2)}) copy-start(bf16[2048,272]{0,1:T(8,128)(2,1)} %all-gather.12.cloned.1.call-done) | copy-start | bytes 3342340
  996.2 150.2 %all-reduce.17.cloned.1.call-start = ((), (), s32[]{:S(2)}) async-start(), calls=%async_computation.35 | async-start | bytes 1392640
  999.1 62.9 %copy-start.21 = (bf16[272,1,816]{2,0,1:T(8,128)(2,1)S(1)}, bf16[272,1,816]{2,0,1:T(8,128)(2,1)}, u32[]{:S(2)}) copy-start(bf16[272,1,816]{2,0,1:T(8,128)(2,1)} %copy-done.20) | copy-start | bytes 1331716
  1061.9 119.7 %reduce-scatter.40.cloned.1.call-start = ((), (), s32[]{:S(2)}) async-start(), calls=%async_computation.31 | async-start | bytes 2785280 | tf_op jit(solution)/shard_map/reduce_scatter | solution.py:68
  1066.6 149.8 %reduce-scatter.30.cloned.1.call-start = ((), (), s32[]{:S(2)}) async-start(), calls=%async_computation.22 | async-start | bytes 2785280 | tf_op jit(solution)/shard_map/reduce_scatter | solution.py:68
  1155.0 61.4 %copy-start.3 = (f32[512,272]{0,1:T(8,128)S(1)}, f32[512,272]{0,1:T(8,128)}, u32[]{:S(2)}) copy-start(f32[512,272]{0,1:T(8,128)} %reduce-scatter.34.cloned.1.call-done) | copy-start | bytes 1671172
  1155.0 61.4 %copy-start.12 = (bf16[512,272]{0,1:T(8,128)(2,1)S(1)}, bf16[512,272]{0,1:T(8,128)(2,1)}, u32[]{:S(2)}) copy-start(bf16[512,272]{0,1:T(8,128)(2,1)} %param.18) | copy-start | bytes 835588
  1155.0 61.4 %copy-start.37 = (f32[512]{0:T(512)S(1)}, f32[512]{0:T(512)}, u32[]{:S(2)}) copy-start(f32[512]{0:T(512)} %copy-done.35) | copy-start | bytes 6148
  1155.0 61.4 %copy-start.40 = (f32[512]{0:T(512)S(1)}, f32[512]{0:T(512)}, u32[]{:S(2)}) copy-start(f32[512]{0:T(512)} %copy-done.38) | copy-start | bytes 6148
  1155.0 61.4 %copy-start.52 = (f32[512]{0:T(512)S(1)}, f32[512]{0:T(512)}, u32[]{:S(2)}) copy-start(f32[512]{0:T(512)} %copy-done.51) | copy-start | bytes 6148
  1155.0 61.4 %copy-start.54 = (f32[512]{0:T(512)S(1)}, f32[512]{0:T(512)}, u32[]{:S(2)}) copy-start(f32[512]{0:T(512)} %copy-done.53) | copy-start | bytes 6148
  (61 other events, 1209.3 us)
Sparse Core Ops, SparseCore 0:
  36.0 15.2 all-gather.11
  60.3 115.3 reduce-scatter.23
  178.3 30.1 all-gather.13
  225.2 28.9 all-gather.15
  257.8 31.7 reduce-scatter.25
  291.1 17.0 all-gather.21
  310.4 17.0 all-gather.17
  330.0 152.7 reduce-scatter.31
  485.3 153.6 reduce-scatter.27
  643.6 85.9 all-gather.23
  735.0 30.6 reduce-scatter.33
  781.5 14.3 all-gather.25
  799.4 45.9 reduce-scatter.35
  866.2 37.6 reduce-scatter.37
  906.0 85.0 all-gather.19
  992.6 65.1 all-gather.27
  1060.5 10.4 reduce-scatter.43
  1073.8 17.9 reduce-scatter.41
  1094.7 15.7 reduce-scatter.45
  1113.8 32.5 all-reduce.16
  1149.1 32.3 reduce-scatter.39
  1184.2 32.2 reduce-scatter.29
where the time goes:
time: 1230 us
  waiting for transfers between devices  875 us (71%)
  blocking collectives  135 us (11%)
  matrix products  70.4 us (6%)
  local copies, waits for them, and re-layouts  65.4 us (5%)
  other arithmetic  47.8 us (4%)
  between operations  18.3 us (1%)
  starting transfers between devices  13.7 us (1%)
    reduce_scatter x4, waiting for transfers between devices, across_rows(): lax.psum_scatter(partial_term(jnp.int32(0), share_rows * lax.axis_size('r...  438 us
    all_gather x4, waiting for transfers between devices, gather_rows(): return lax.all_gather(tokens_block, 'row', axis=0, tiled=True)  226 us
    reduce_scatter x4, waiting for transfers between devices, across_cols(): lax.psum_scatter(partial_term(jnp.int32(0), share_rows * lax.axis_size('c...  90.2 us
    psum x4, blocking collectives, feature_sums(): return lax.psum((first_sum, second_sum), 'row')  47.5 us
    dot_general x8, matrix products, weigh(): lax.dot_general(row_block, weight, (((1,), (1 if transposed else 0,)), ((...  43.4 us
    unnamed x26, waiting for transfers between devices  39.7 us
    reduce_scatter x1, waiting for transfers between devices, on_device(): lax.psum_scatter(grad_whole.astype(jnp.bfloat16), 'col', scatter_dimensio...  37.2 us
    unnamed x175, local copies, waits for them, and re-layouts  36.7 us
  transfers between devices with their start and end apart: 22, of which 18 were waited for; matrix products, arithmetic and copies ran while one was open for 10% of the time, Pallas kernels for 0%

commit v1 on v0

v1 whole, which is shorter than its diff:
```python
import jax
import jax.numpy as jnp
from jax import lax
from jax.sharding import PartitionSpec as P

D = 1088
H = 17
HD = 64
STEP = 3
EXT = 320
HALO = 48


NORM_EPS = 1e-05
BETA_ONE = 0.9
BETA_TWO = 0.95
LEARN_RATE = 0.05
VECTOR_RATE = 0.2
DECAY_RATE = 0.1
ADAM_EPS = 1e-08


def gelu_tanh(values_in):
    return jax.nn.gelu(values_in, approximate=True)


def weigh(row_block, weight, transposed):
    return lax.dot_general(
        row_block,
        weight,
        (((1,), (1 if transposed else 0,)), ((), ())),
        preferred_element_type=jnp.float32,
    )


def outer_sum(left_rows, right_rows):
    return lax.dot_general(
        left_rows, right_rows, (((0,), (0,)), ((), ())), preferred_element_type=jnp.float32
    )


def swap_grid(block):
    count = lax.axis_size("row")
    pairs = [(r * count + c, c * count + r) for r in range(count) for c in range(count)]
    return lax.ppermute(block, ("row", "col"), pairs)


def row_stats(values_in):
    row_mean = jnp.mean(values_in, axis=1, keepdims=True)
    spread = jnp.mean(values_in * values_in, axis=1, keepdims=True) - row_mean * row_mean
    return row_mean, lax.rsqrt(spread + NORM_EPS)


def norm_backward(upstream, centred, inv_scale, gain_row):
    pushed = upstream * gain_row
    row_total = jnp.mean(pushed, axis=1, keepdims=True)
    cross = jnp.mean(pushed * centred, axis=1, keepdims=True)
    result = inv_scale * (pushed - row_total - centred * cross)
    return (result, jnp.sum(upstream * centred, axis=0), jnp.sum(upstream, axis=0))


def reduce_rows(grad):
    return lax.psum_scatter(grad, "row", scatter_dimension=0, tiled=True)


def reduce_groups(grad, dim):
    count = lax.axis_size("dp")
    if count != 2:
        return lax.psum_scatter(grad, "dp", scatter_dimension=dim, tiled=True)
    half = grad.shape[dim] // 2
    mine = lax.axis_index("dp")
    kept = lax.dynamic_slice_in_dim(grad, mine * half, half, dim)
    sent = lax.dynamic_slice_in_dim(grad, (1 - mine) * half, half, dim)
    return kept.astype(jnp.float32) + lax.ppermute(sent, "dp", [(0, 1), (1, 0)]).astype(jnp.float32)


def split_heads(columns):
    rows = columns.shape[0]
    return columns.reshape(rows, EXT // HD, HD).transpose(1, 0, 2)


def join_heads(heads):
    return heads.transpose(1, 0, 2).reshape(heads.shape[1], EXT)


def batched(spec, left, right):
    return jnp.einsum(spec, left, right, preferred_element_type=jnp.float32)


def adam_step(master, moment, gradient, decay_rate, step_rate):
    first_moment = BETA_ONE * moment[0] + (1.0 - BETA_ONE) * gradient
    second_moment = BETA_TWO * moment[1] + (1.0 - BETA_TWO) * gradient * gradient
    change = (
        first_moment
        / (1.0 - BETA_ONE**STEP)
        / (jnp.sqrt(second_moment / (1.0 - BETA_TWO**STEP)) + ADAM_EPS)
    )
    change = change + decay_rate * master
    return (master - step_rate * change, jnp.stack([first_moment, second_moment]))


def on_device(
    block_in,
    cotangent,
    lengths,
    qkv_weight,
    proj_weight,
    fc1_weight,
    fc2_weight,
    qkv_bias,
    fc1_bias,
    row_vectors,
    qkv_moments,
    proj_moments,
    fc1_moments,
    fc2_moments,
    qkv_bias_moments,
    fc1_bias_moments,
    row_moments,
):
    wide = jnp.float32
    short = jnp.bfloat16
    my_col = lax.axis_index("col")
    my_row = lax.axis_index("row")
    my_dp = lax.axis_index("dp")
    n_dp = lax.axis_size("dp")
    n_col = lax.axis_size("col")
    n_row = lax.axis_size("row")
    part = D // n_col
    pack_len = block_in.shape[0]

    x_part = swap_grid(block_in)
    x_bf = lax.all_gather(x_part, "col", axis=1, tiled=True)
    cot_part = swap_grid(cotangent)
    cot = lax.all_gather(cot_part, "col", axis=1, tiled=True)

    small = jnp.concatenate(
        [row_vectors.reshape(-1), fc1_bias.reshape(-1), qkv_bias.reshape(-1)]
    ).astype(short)
    rv_size = row_vectors.size
    b1_size = fc1_bias.size
    small_all = lax.all_gather(small, ("row", "col", "dp"), axis=0, tiled=False)
    small_all = small_all.reshape(n_row, n_col, n_dp, small.shape[0]).astype(wide)
    vectors = (
        small_all[:, 0, :, :rv_size]
        .reshape(n_row, n_dp, 6, part // n_dp)
        .transpose(2, 0, 1, 3)
        .reshape(6, D)
    )
    bias_fc1 = lax.dynamic_index_in_dim(
        small_all[0, :, :, rv_size : rv_size + b1_size], my_col, 0, keepdims=False
    ).reshape(-1)
    bias_qkv_all = small_all[0, :, :, rv_size + b1_size :].reshape(3, D)

    ext_start = my_col * (EXT - HD)
    own_start = my_col * (part - (EXT - HD))
    qkv_cols = lax.all_gather(
        qkv_weight[:, 0, :].astype(short), ("col", "dp"), axis=1, tiled=True
    )
    qkv_ext = jnp.concatenate(
        [lax.dynamic_slice_in_dim(qkv_cols, i * D + ext_start, EXT, 1) for i in range(3)], axis=1
    )
    w_qkv = lax.all_gather(qkv_ext, "row", axis=0, tiled=True)
    bias_qkv = lax.dynamic_slice_in_dim(bias_qkv_all, ext_start, EXT, 1).reshape(-1)

    proj_t = proj_weight[:, 0, :].astype(short).T
    halo = HALO
    from_left = lax.ppermute(
        proj_t[:, part - halo :], "col", [(i, i + 1) for i in range(n_col - 1)]
    )
    from_right = lax.ppermute(proj_t[:, :halo], "col", [(i + 1, i) for i in range(n_col - 1)])
    proj_ext = lax.dynamic_slice_in_dim(
        jnp.concatenate([from_left, proj_t, from_right], axis=1), halo - own_start, EXT, 1
    )
    w_proj_t = lax.all_gather(proj_ext, ("row", "dp"), axis=0, tiled=True)
    fc1_cols = lax.all_gather(fc1_weight[:, 0, :].astype(short), "dp", axis=1, tiled=True)
    w_fc1 = lax.all_gather(fc1_cols, "row", axis=0, tiled=True)
    w_fc2_t = lax.all_gather(
        fc2_weight[:, 0, :].astype(short).T, ("row", "dp"), axis=0, tiled=True
    )

    x_full = x_bf.astype(wide)
    mean_one, scale_one = row_stats(x_full)
    centred_one = (x_full - mean_one) * scale_one
    normed_one = (centred_one * vectors[0] + vectors[1]).astype(short)
    mixed = (weigh(normed_one, w_qkv, False) + bias_qkv).astype(short)
    queries = split_heads(mixed[:, :EXT])
    keys = split_heads(mixed[:, EXT : 2 * EXT])
    values = split_heads(mixed[:, 2 * EXT :])
    seq_ends = jnp.cumsum(lengths[0])
    places = jnp.arange(pack_len, dtype=jnp.int32)
    segment = jnp.sum((places[:, None] >= seq_ends[None, :]).astype(jnp.int32), axis=1)
    allowed = (segment[:, None] == segment[None, :]) & (places[None, :] <= places[:, None])
    scores = jnp.where(
        allowed[None], batched("hqd,hkd->hqk", queries, keys) * HD ** (-0.5), -1e30
    )
    row_top = jnp.max(scores, axis=2, keepdims=True)
    log_total = row_top + jnp.log(jnp.sum(jnp.exp(scores - row_top), axis=2, keepdims=True))
    probs = jnp.exp(scores - log_total)
    weights = probs.astype(short)
    attended = batched("hqk,hkd->hqd", weights, values).astype(short)
    own = jnp.arange(EXT)
    own = (own >= own_start) & (own < own_start + part)
    att_own = jnp.where(own[None, :], join_heads(attended), 0).astype(short)
    x_mid = (
        x_full
        + lax.psum(weigh(att_own, w_proj_t, True).astype(short), "col").astype(wide)
        + vectors[2]
    )

    mean_two, scale_two = row_stats(x_mid)
    centred_two = (x_mid - mean_two) * scale_two
    normed_two = (centred_two * vectors[3] + vectors[4]).astype(short)
    pre_act = weigh(normed_two, w_fc1, False) + bias_fc1
    hidden = gelu_tanh(pre_act).astype(short)
    out_part = lax.psum_scatter(
        weigh(hidden, w_fc2_t, True).astype(short), "col", scatter_dimension=1, tiled=True
    ).astype(wide)
    mid_part = lax.dynamic_slice_in_dim(x_mid, my_col * part, part, 1)
    shift_part = lax.dynamic_slice_in_dim(vectors[5], my_col * part, part, 0)
    block_out = swap_grid((mid_part + out_part + shift_part).astype(short))

    grad_hidden = weigh(cot, w_fc2_t, False)
    grad_pre = jax.vjp(gelu_tanh, pre_act)[1](grad_hidden)[0].astype(short)
    grad_fc2_t = outer_sum(cot, hidden).astype(short)
    shard_fc2 = reduce_groups(reduce_rows(grad_fc2_t), 0)
    grad_fc1 = outer_sum(normed_two, grad_pre).astype(short)
    shard_fc1 = reduce_groups(reduce_rows(grad_fc1), 1)
    cot_wide = cot.astype(wide)
    grad_bias_two = jnp.sum(cot_wide, axis=0)
    grad_bias_fc1 = jnp.sum(grad_pre.astype(wide), axis=0)
    grad_normed_two = lax.psum(weigh(grad_pre, w_fc1, True).astype(short), "col").astype(wide)
    back_two, gain_two, shift_two = norm_backward(
        grad_normed_two, centred_two, scale_two, vectors[3]
    )
    grad_mid = cot_wide + back_two
    grad_mid_short = grad_mid.astype(short)
    grad_bias_proj = jnp.sum(grad_mid_short.astype(wide), axis=0)
    grad_proj_t = lax.dynamic_slice_in_dim(
        outer_sum(grad_mid_short, att_own).astype(short), own_start, part, 1
    )
    shard_proj = reduce_groups(reduce_rows(grad_proj_t), 0)
    grad_att = split_heads(weigh(grad_mid_short, w_proj_t, False).astype(short))
    grad_values = batched("hqk,hqd->hkd", weights, grad_att)
    grad_probs = batched("hqd,hkd->hqk", grad_att, values)
    delta = jnp.sum(grad_att.astype(wide) * attended.astype(wide), axis=2, keepdims=True)
    grad_scores = (probs * (grad_probs - delta) * HD ** (-0.5)).astype(short)
    grad_query = batched("hqk,hkd->hqd", grad_scores, keys)
    grad_keys = batched("hqk,hqd->hkd", grad_scores, queries)
    units = [
        lax.dynamic_slice_in_dim(join_heads(grad.astype(short)), own_start, part, 1)
        for grad in (grad_query, grad_keys, grad_values)
    ]
    grad_ext = jnp.concatenate(
        [
            jnp.where(own[None, :], join_heads(grad.astype(short)), 0).astype(short)
            for grad in (grad_query, grad_keys, grad_values)
        ],
        axis=1,
    )
    stacked = jnp.stack(units)
    picks = [
        lax.dynamic_index_in_dim(stacked, jnp.array(table)[my_col], 0, keepdims=False)
        for table in ((0, 1, 1, 2), (1, 0, 2, 1), (2, 2, 0, 0))
    ]
    unit_b = lax.ppermute(picks[1], "col", [(0, 1), (1, 0), (2, 3), (3, 2)])
    unit_c = lax.ppermute(picks[2], "col", [(0, 2), (2, 0), (1, 3), (3, 1)])
    odd = (my_col % 2) == 1
    grad_block = jnp.concatenate(
        [jnp.where(odd, unit_c, picks[0]), unit_b, jnp.where(odd, picks[0], unit_c)], axis=1
    )
    grad_normed_one = lax.psum(weigh(grad_ext, w_qkv, True).astype(short), "col").astype(wide)
    grad_qkv = outer_sum(normed_one, grad_block).astype(short)
    shard_qkv = reduce_groups(reduce_rows(grad_qkv), 1)
    grad_bias_qkv = jnp.sum(grad_block.astype(wide), axis=0)
    back_one, gain_one, shift_one = norm_backward(
        grad_normed_one, centred_one, scale_one, vectors[0]
    )
    in_grad = lax.dynamic_slice_in_dim(grad_mid + back_one, my_col * part, part, 1)
    block_in_grad = swap_grid(in_grad.astype(short)).astype(wide)

    row_grads = jnp.stack(
        [gain_one, shift_one, grad_bias_proj, gain_two, shift_two, grad_bias_two]
    )
    sums = lax.psum(
        jnp.concatenate([row_grads.reshape(-1), grad_bias_fc1, grad_bias_qkv]), ("row", "dp")
    )
    vec_size = part // n_dp
    row_shard = lax.dynamic_slice_in_dim(
        sums[: 6 * D].reshape(6, D), my_row * part + my_dp * vec_size, vec_size, 1
    )[:, None, :]
    fc1_bias_shard = lax.dynamic_slice_in_dim(
        sums[6 * D : 6 * D + grad_bias_fc1.shape[0]], my_dp * b1_size, b1_size, 0
    )[None, :]
    qkv_bias_shard = lax.dynamic_slice_in_dim(
        sums[6 * D + grad_bias_fc1.shape[0] :], my_dp * qkv_bias.size, qkv_bias.size, 0
    )[None, :]
    grads = (
        shard_qkv.astype(wide)[:, None, :],
        shard_proj.astype(wide).T[:, None, :],
        shard_fc1.astype(wide)[:, None, :],
        shard_fc2.astype(wide).T[:, None, :],
        qkv_bias_shard,
        fc1_bias_shard,
        row_shard,
    )
    masters = (qkv_weight, proj_weight, fc1_weight, fc2_weight, qkv_bias, fc1_bias, row_vectors)
    moments = (
        qkv_moments,
        proj_moments,
        fc1_moments,
        fc2_moments,
        qkv_bias_moments,
        fc1_bias_moments,
        row_moments,
    )
    decays = (DECAY_RATE, DECAY_RATE, DECAY_RATE, DECAY_RATE, 0.0, 0.0, 0.0)
    rates = (LEARN_RATE, LEARN_RATE, LEARN_RATE, LEARN_RATE, VECTOR_RATE, VECTOR_RATE, VECTOR_RATE)
    updates = [
        adam_step(master, moment, gradient, decay_rate, step_rate)
        for master, moment, gradient, decay_rate, step_rate in zip(
            masters, moments, grads, decays, rates
        )
    ]
    return (
        block_out,
        block_in_grad,
        grads[0],
        grads[1],
        grads[2],
        grads[3],
        grads[4],
        grads[5],
        grads[6],
        updates[0][0],
        updates[1][0],
        updates[2][0],
        updates[3][0],
        updates[4][0],
        updates[5][0],
        updates[6][0],
        updates[0][1],
        updates[1][1],
        updates[2][1],
        updates[3][1],
        updates[4][1],
        updates[5][1],
        updates[6][1],
    )


def solution(mesh):
    in_specs = (
        P(("dp", "col"), "row"),
        P(("dp", "col"), "row"),
        P(("dp", "row"), None),
        P("row", "col", "dp"),
        P("col", "row", "dp"),
        P("row", "col", "dp"),
        P("col", "row", "dp"),
        P("col", "dp"),
        P("col", "dp"),
        P(None, "row", "dp"),
        P(None, "row", "col", "dp"),
        P(None, "col", "row", "dp"),
        P(None, "row", "col", "dp"),
        P(None, "col", "row", "dp"),
        P(None, "col", "dp"),
        P(None, "col", "dp"),
        P(None, None, "row", "dp"),
    )
    out_specs = (
        P(("dp", "col"), "row"),
        P(("dp", "col"), "row"),
        P("row", "col", "dp"),
        P("col", "row", "dp"),
        P("row", "col", "dp"),
        P("col", "row", "dp"),
        P("col", "dp"),
        P("col", "dp"),
        P(None, "row", "dp"),
        P("row", "col", "dp"),
        P("col", "row", "dp"),
        P("row", "col", "dp"),
        P("col", "row", "dp"),
        P("col", "dp"),
        P("col", "dp"),
        P(None, "row", "dp"),
        P(None, "row", "col", "dp"),
        P(None, "col", "row", "dp"),
        P(None, "row", "col", "dp"),
        P(None, "col", "row", "dp"),
        P(None, "col", "dp"),
        P(None, "col", "dp"),
        P(None, None, "row", "dp"),
    )
    return jax.shard_map(
        on_device, mesh=mesh, in_specs=in_specs, out_specs=out_specs, check_vma=False
    )
```

time: 1230 us -> 720 us (0.59)
  waiting for transfers between devices: 875 us -> 321 us
  local copies, waits for them, and re-layouts: 65.4 us -> 99.3 us
  matrix products: 70.4 us -> 49.1 us
  blocking collectives: 135 us -> 154 us
    reduce_scatter x9 -> x3, waiting for transfers between devices: 566 us -> 46.3 us  [the longest x2 46.3 us: reduce_rows(): return lax.psum_scatter(grad, 'row', scatter_dimension=0, tiled=True)]
    all_gather x9 -> x6, waiting for transfers between devices: 270 us -> 164 us  [the longest x1 56.6 us: on_device(): lax.all_gather(fc2_weight[:, 0, :].astype(short).T, ('row', 'dp'), axis=0...]
    all_gather x5 -> x3, blocking collectives: 50.8 us -> 115 us  [the longest x1 69.7 us: on_device(): small_all = lax.all_gather(small, ('row', 'col', 'dp'), axis=0, tiled=False)]
    psum x0 -> x3, waiting for transfers between devices: none -> 47.7 us  [the longest x1 34.9 us: on_device(): lax.psum(weigh(grad_pre, w_fc1, True).astype(short), 'col').astype(wide)]
    unnamed x175 -> x188, local copies, waits for them, and re-layouts: 36.7 us -> 55.2 us
    all_to_all x2 -> x0, blocking collectives: 17.3 us -> none  [the longest x1 8.73 us: on_device(): lax.all_to_all(grad_heads, 'col', split_axis=0, concat_axis=1, tiled=True)]
    ppermute x0 -> x12, waiting for transfers between devices: none -> 16 us  [the longest x1 8.85 us: on_device(): unit_c = lax.ppermute(picks[2], 'col', [(0, 2), (2, 0), (1, 3), (3, 1)])]
    ppermute x0 -> x12, starting transfers between devices: none -> 15.7 us  [the longest x4 6.73 us: swap_grid(): return lax.ppermute(block, ('row', 'col'), pairs)]
  transfers between devices with their start and end apart: 22 -> 26, of which waited for: 18 -> 12; matrix products, arithmetic and copies ran while one was open for 10% -> 19% of each run, Pallas kernels for 0% -> 0%
where the time goes in v1:
time: 720 us; the launch traced here: 712 us
  waiting for transfers between devices  321 us (45%)
  blocking collectives  154 us (21%)
  local copies, waits for them, and re-layouts  99.3 us (14%)
  other arithmetic  50.8 us (7%)
  matrix products  49.1 us (7%)
  between operations  21.3 us (3%)
  starting transfers between devices  17.1 us (2%)
    all_gather x1, blocking collectives, on_device(): small_all = lax.all_gather(small, ('row', 'col', 'dp'), axis=0, tiled=False)  69.7 us
    all_gather x1, waiting for transfers between devices, on_device(): lax.all_gather(fc2_weight[:, 0, :].astype(short).T, ('row', 'dp'), axis=0...  56.6 us
    unnamed x188, local copies, waits for them, and re-layouts  55.2 us
    all_gather x1, waiting for transfers between devices, on_device(): w_fc1 = lax.all_gather(fc1_cols, 'row', axis=0, tiled=True)  49.9 us
    reduce_scatter x2, waiting for transfers between devices, reduce_rows(): return lax.psum_scatter(grad, 'row', scatter_dimension=0, tiled=True)  46.3 us
    unnamed x16, waiting for transfers between devices  46.2 us
    all_gather x1, waiting for transfers between devices, on_device(): lax.all_gather(qkv_weight[:, 0, :].astype(short), ('col', 'dp'), axis=1,...  44.9 us
    psum x1, blocking collectives, on_device(): lax.psum(jnp.concatenate([row_grads.reshape(-1), grad_bias_fc1, grad_bias...  38.4 us
  transfers between devices with their start and end apart: 26, of which 12 were waited for; matrix products, arithmetic and copies ran while one was open for 19% of the time, Pallas kernels for 0%

profile of v1, /device:TPU:0, one launch (start us, length us, event | category | flops | bytes accessed | tf_op | source)
XLA Modules:
  0.0 712.1 jit_solution(14864568885283516891)
XLA Ops:
  11.7 44.9 %all-gather.19.cloned.1.call-done = bf16[272,1,3264]{0,1,2:T(2,128)(2,1)} async-done(((bf16[272,1,408]{0,1,2:T(2,128)(2,1)}), bf16[272,1,3264]{0,1,2:T(2,128)(2,1)}) %all-gather.19.cloned.1.call-update) | async-done | bytes 1775632 | tf_op jit(solution)/shard_map/all_gather | solution.py:157
  56.6 2.8 constant_dynamic-slice_fusion.11
  64.5 3.0 collective-permute-start.1
  67.8 69.7 %all-gather.3 = bf16[32,1,1768]{2,1,0:T(2,128)(2,1)S(1)} all-gather(bf16[1,1,1768]{2,1,0:T(2,128)(2,1)S(1)} %bitcast.264), channel_id=1, replica_groups=mesh['dp'=2,'row'=4,'col'=4] {'row','col','dp'}, dimensions={0}, use_global_device_ids=true | all-gather | bytes 116688 | tf_op jit(solution)/shard_map/all_gather | solution.py:142
  140.4 32.5 %all_gather.32 = bf16[1088,320]{1,0:T(8,128)(2,1)S(1)} all-gather(bf16[136,320]{1,0:T(8,128)(2,1)S(1)} %dynamic-slice_maximum_fusion), channel_id=1, replica_groups=mesh['dp'=2,'row'=4,'col'=4] {'row','dp'}, dimensions={0}, use_global_device_ids=true | all-gather | bytes 783360 | tf_op jit(solution)/shard_map/all_gather | solution.py:175
  174.8 3.7 add_convert_fusion.2
  186.9 13.3 %all-gather.1 = bf16[272,1,1088]{0,1,2:T(2,128)(2,1)S(1)} all-gather(bf16[272,1,544]{0,1,2:T(2,128)(2,1)S(1)} %copy.305), channel_id=3, replica_groups=mesh['dp'=2,'row'=4,'col'=4] {'dp'}, dimensions={2}, use_global_device_ids=true | all-gather | bytes 887808 | tf_op jit(solution)/shard_map/all_gather | solution.py:176
  200.2 3.7 copy.306
  211.1 12.8 %all-reduce.4.cloned.1.call-done = bf16[512,1088]{0,1:T(8,128)(2,1)} async-done(((bf16[512,1088]{0,1:T(8,128)(2,1)}), bf16[512,1088]{0,1:T(8,128)(2,1)}) %all-reduce.4.cloned.1.call-update) | async-done | bytes 1114128 | tf_op jit(solution)/shard_map/psum | solution.py:207
  226.3 49.9 %all-gather.21.cloned.1.call-done = bf16[1088,1,1088]{2,0,1:T(8,128)(2,1)} async-done(((bf16[272,1,1088]{2,0,1:T(8,128)(2,1)}), bf16[1088,1,1088]{2,0,1:T(8,128)(2,1)}) %all-gather.21.cloned.1.call-update) | async-done | bytes 2367504 | tf_op jit(solution)/shard_map/all_gather | solution.py:177
  276.3 5.1 convolution_add_fusion
  281.3 12.9 %all-gather.17.cloned.1.call-done = bf16[512,1088]{0,1:T(8,128)(2,1)} async-done(((bf16[512,272]{0,1:T(8,128)(2,1)}), bf16[512,1088]{0,1:T(8,128)(2,1)}) %all-gather.17.cloned.1.call-update) | async-done | bytes 1114128 | tf_op jit(solution)/shard_map/all_gather | solution.py:135
  294.2 56.6 %all-gather.15.cloned.1.call-done = bf16[1088,1088]{1,0:T(8,128)(2,1)} async-done(((bf16[136,1088]{1,0:T(8,128)(2,1)}), bf16[1088,1088]{1,0:T(8,128)(2,1)}) %all-gather.15.cloned.1.call-update) | async-done | bytes 2367504 | tf_op jit(solution)/shard_map/all_gather | solution.py:178
  350.8 6.5 convert_reduce_fusion.4
  358.3 2.6 convolution_convert_fusion.3
  361.4 34.9 %all-reduce.6.cloned.1.call-done = bf16[512,1088]{0,1:T(8,128)(2,1)} async-done(((bf16[512,1088]{0,1:T(8,128)(2,1)}), bf16[512,1088]{0,1:T(8,128)(2,1)}) %all-reduce.6.cloned.1.call-update) | async-done | bytes 1114128 | tf_op jit(solution)/shard_map/psum | solution.py:232
  396.3 3.1 fusion.18
  399.4 3.6 convert_reduce_fusion.5
  419.1 5.2 convolution_convert_fusion.4
  440.0 8.9 %collective-permute-done.6 = bf16[512,272]{0,1:T(8,128)(2,1)} collective-permute-done((bf16[512,272]{0,1:T(8,128)(2,1)}, bf16[512,272]{0,1:T(8,128)(2,1)}, u32[]{:S(2)}, u32[]{:S(2)}) %collective-permute-start.6) | collective-permute-done | bytes 278560 | tf_op jit(solution)/shard_map/ppermute | solution.py:267
  450.7 3.7 convolution_convert_fusion.2
  454.5 4.6 convolution_convert_fusion.1
  476.5 3.1 fusion.87
  481.6 3.6 fusion
  485.2 5.1 copy.354
  492.5 4.1 fusion.19
  497.0 38.4 %psum.31 = f32[8432]{0:T(1024)S(1)} all-reduce(f32[8432]{0:T(1024)S(1)} %concatenate.34), channel_id=1, replica_groups=mesh['dp'=2,'row'=4,'col'=4] {'row','dp'}, use_global_device_ids=true, to_apply=%region_29.30 | all-reduce | flops 8432 | bytes 67456 | tf_op jit(solution)/shard_map/psum | solution.py:285
  547.9 2.7 collective-permute-done.9
  555.1 4.0 collective-permute-start.3
  571.8 46.3 %reduce-scatter.14.cloned.1.call-done = bf16[272,1088]{1,0:T(8,128)(2,1)} async-done(((bf16[1088,1088]{1,0:T(8,128)(2,1)}), bf16[272,1088]{1,0:T(8,128)(2,1)}) %reduce-scatter.14.cloned.1.call-update) | async-done | bytes 591888 | tf_op jit(solution)/shard_map/reduce_scatter | solution.py:63
  626.8 45.9 %reduce-scatter.18.cloned.1.call-done = bf16[272,1088]{1,0:T(8,128)(2,1)} async-done(((bf16[1088,1088]{1,0:T(8,128)(2,1)}), bf16[272,1088]{1,0:T(8,128)(2,1)}) %reduce-scatter.18.cloned.1.call-update) | async-done | bytes 591888
  680.9 2.9 collective-permute-done.11
  (367 shorter events, 150.6 us)
Async XLA Ops:
  7.2 49.4 %all-gather.19.cloned.1.call-start = ((), (), s32[]{:S(2)}) async-start(), calls=%async_computation.15 | async-start | bytes 5640192 | tf_op jit(solution)/shard_map/all_gather | solution.py:157
  10.2 162.7 %all-gather.11.cloned.1.call-start = ((), (), s32[]{:S(2)}) async-start(), calls=%async_computation.5 | async-start | bytes 1392640 | tf_op jit(solution)/shard_map/all_gather | solution.py:133
  10.2 0.7 collective-permute-start
  11.7 163.1 %all-gather.13.cloned.1.call-start = ((), (), s32[]{:S(2)}) async-start(), calls=%async_computation.6 | async-start | bytes 2785280 | tf_op jit(solution)/shard_map/all_gather | solution.py:163
  61.2 77.4 %copy-start.74 = (s32[1,3]{1,0:T(1,128)S(1)}, s32[1,3]{1,0:T(1,128)}, u32[]{:S(2)}) copy-start(s32[1,3]{1,0:T(1,128)} %param.22) | copy-start | bytes 40
  63.0 160.9 %all-reduce.4.cloned.1.call-start = ((), (), s32[]{:S(2)}) async-start(), calls=%async_computation.7 | async-start | bytes 2228224 | tf_op jit(solution)/shard_map/psum | solution.py:207
  63.2 77.0 %collective-permute-start.2 = (bf16[136,48]{1,0:T(8,128)(2,1)S(1)}, bf16[136,48]{1,0:T(8,128)(2,1)S(1)}, u32[]{:S(2)}, u32[]{:S(2)}) collective-permute-start(bf16[136,48]{1,0:T(8,128)(2,1)S(1)} %get-tuple-element.255), channel_id=1, source_target_pairs={{1,0},{2,1},{3,2},{5,4},{6,5},{7,6},{9,8},{10,9},{11,10},{13,12},{... | collective-permute-start | bytes 39176 | tf_op jit(solution)/shard_map/ppermute | solution.py:171
  64.5 75.7 %collective-permute-start.1 = (bf16[136,48]{1,0:T(8,128)(2,1)S(1)}, bf16[136,48]{1,0:T(8,128)(2,1)S(1)}, u32[]{:S(2)}, u32[]{:S(2)}) collective-permute-start(bf16[136,48]{1,0:T(8,128)(2,1)S(1)} %get-tuple-element.254), channel_id=1, source_target_pairs={{0,1},{1,2},{2,3},{4,5},{5,6},{6,7},{8,9},{9,10},{10,11},{12,13},{... | collective-permute-start | bytes 39176 | tf_op jit(solution)/shard_map/ppermute | solution.py:168
  185.5 90.8 %all-gather.21.cloned.1.call-start = ((), (), s32[]{:S(2)}) async-start(), calls=%async_computation.16 | async-start | bytes 3133440 | tf_op jit(solution)/shard_map/all_gather | solution.py:177
  203.9 90.3 %all-gather.17.cloned.1.call-start = ((), (), s32[]{:S(2)}) async-start(), calls=%async_computation.10 | async-start | bytes 1392640 | tf_op jit(solution)/shard_map/all_gather | solution.py:135
  203.9 0.7 collective-permute-start.4
  205.4 145.4 %all-gather.15.cloned.1.call-start = ((), (), s32[]{:S(2)}) async-start(), calls=%async_computation.8 | async-start | bytes 2820096 | tf_op jit(solution)/shard_map/all_gather | solution.py:178
  207.3 189.0 %all-reduce.6.cloned.1.call-start = ((), (), s32[]{:S(2)}) async-start(), calls=%async_computation.11 | async-start | bytes 2228224 | tf_op jit(solution)/shard_map/psum | solution.py:232
  360.9 131.6 %all-reduce.8.cloned.1.call-start = ((), (), s32[]{:S(2)}) async-start(), calls=%async_computation.12 | async-start | bytes 2228224 | tf_op jit(solution)/shard_map/psum | solution.py:272
  413.6 130.0 %reduce-scatter.16.cloned.1.call-start = ((), (), s32[]{:S(2)}) async-start(), calls=%async_computation.17 | async-start | bytes 1044480
  419.1 134.2 %reduce-scatter.10.cloned.1.call-start = ((), (), s32[]{:S(2)}) async-start(), calls=%async_computation.9 | async-start | bytes 1392640 | tf_op jit(solution)/shard_map/reduce_scatter | solution.py:216
  424.3 134.8 %reduce-scatter.12.cloned.1.call-start = ((), (), s32[]{:S(2)}) async-start(), calls=%async_computation.13 | async-start | bytes 2437120 | tf_op jit(solution)/shard_map/reduce_scatter | solution.py:63
  435.8 13.1 %collective-permute-start.6 = (bf16[512,272]{0,1:T(8,128)(2,1)}, bf16[512,272]{0,1:T(8,128)(2,1)}, u32[]{:S(2)}, u32[]{:S(2)}) collective-permute-start(bf16[512,272]{0,1:T(8,128)(2,1)} %get-tuple-element.242), channel_id=1, source_target_pairs={{0,2},{2,0},{1,3},{3,1},{4,6},{6,4},{5,7},{7,5},{8,10},{10,8},{9,1... | collective-permute-start | bytes 835592 | tf_op jit(solution)/shard_map/ppermute | solution.py:267
  436.8 13.2 %collective-permute-start.7 = (bf16[512,272]{0,1:T(8,128)(2,1)}, bf16[512,272]{0,1:T(8,128)(2,1)}, u32[]{:S(2)}, u32[]{:S(2)}) collective-permute-start(bf16[512,272]{0,1:T(8,128)(2,1)} %get-tuple-element.241), channel_id=1, source_target_pairs={{0,1},{1,0},{2,3},{3,2},{4,5},{5,4},{6,7},{7,6},{8,9},{9,8},{10,11... | collective-permute-start | bytes 835592 | tf_op jit(solution)/shard_map/ppermute | solution.py:266
  454.5 163.6 %reduce-scatter.14.cloned.1.call-start = ((), (), s32[]{:S(2)}) async-start(), calls=%async_computation.14 | async-start | bytes 3133440 | tf_op jit(solution)/shard_map/reduce_scatter | solution.py:63
  459.1 213.6 %reduce-scatter.18.cloned.1.call-start = ((), (), s32[]{:S(2)}) async-start(), calls=%async_computation.18 | async-start | bytes 3133440
  496.7 53.9 %copy-start.22 = (f32[1,272,1,136]{3,1,2,0:T(8,128)S(1)}, f32[1,272,1,136]{3,1,2,0:T(8,128)}, u32[]{:S(2)}) copy-start(f32[1,272,1,136]{3,1,2,0:T(8,128)} %copy.366) | copy-start | bytes 443908
  496.7 53.9 %copy-start.23 = (f32[1,272,1,136]{3,1,2,0:T(8,128)S(1)}, f32[1,272,1,136]{3,1,2,0:T(8,128)}, u32[]{:S(2)}) copy-start(f32[1,272,1,136]{3,1,2,0:T(8,128)} %copy.367) | copy-start | bytes 443908
  537.1 8.9 %collective-permute-start.5 = (bf16[512,272]{0,1:T(8,128)(2,1)S(1)}, bf16[512,272]{0,1:T(8,128)(2,1)}, u32[]{:S(2)}, u32[]{:S(2)}) collective-permute-start(bf16[512,272]{0,1:T(8,128)(2,1)S(1)} %fusion.41), channel_id=1, source_target_pairs={{0,0},{1,4},{2,8},{3,12},{4,1},{5,5},{6,9},{7,13},{8,2},{9,6},{10,... | collective-permute-start | bytes 835592 | tf_op jit(solution)/shard_map/ppermute | solution.py:45
  545.3 5.3 collective-permute-start.9
  555.1 11.2 %collective-permute-start.3 = (bf16[512,272]{0,1:T(8,128)(2,1)}, bf16[512,272]{0,1:T(8,128)(2,1)}, u32[]{:S(2)}, u32[]{:S(2)}) collective-permute-start(bf16[512,272]{0,1:T(8,128)(2,1)} %add_convert_fusion.3), channel_id=1, source_target_pairs={{0,0},{1,4},{2,8},{3,12},{4,1},{5,5},{6,9},{7,13},{8,2},{9,6},{10,... | collective-permute-start | bytes 835592 | tf_op jit(solution)/shard_map/ppermute | solution.py:45
  561.0 6.9 collective-permute-start.8
  620.0 56.3 %collective-permute-start.10 = (bf16[272,544]{1,0:T(8,128)(2,1)}, bf16[272,544]{1,0:T(8,128)(2,1)S(1)}, u32[]{:S(2)}, u32[]{:S(2)}) collective-permute-start(bf16[272,544]{1,0:T(8,128)(2,1)} %constant_dynamic-slice_fusion.3), channel_id=1, source_target_pairs={{0,16},{16,0},{1,17},{17,1},{2,18},{18,2},{3,19},{19,3},{4,20},{20... | collective-permute-start | bytes 887816 | tf_op jit(solution)/shard_map/ppermute | solution.py:74
  624.6 52.3 %copy-start.7 = (f32[1,272,1,544]{3,2,1,0:T(1,128)S(1)}, f32[1,272,1,544]{3,2,1,0:T(1,128)}, u32[]{:S(2)}) copy-start(f32[1,272,1,544]{3,2,1,0:T(1,128)} %get-tuple-element.222) | copy-start | bytes 1775620
  624.6 52.3 %copy-start.8 = (f32[1,272,1,544]{3,2,1,0:T(1,128)S(1)}, f32[1,272,1,544]{3,2,1,0:T(1,128)}, u32[]{:S(2)}) copy-start(f32[1,272,1,544]{3,2,1,0:T(1,128)} %get-tuple-element.223) | copy-start | bytes 1775620
  624.6 52.3 %copy-start.27 = (bf16[272,1088]{1,0:T(8,128)(2,1)S(1)}, bf16[272,1088]{1,0:T(8,128)(2,1)}, u32[]{:S(2)}) copy-start(bf16[272,1088]{1,0:T(8,128)(2,1)} %reduce-scatter.14.cloned.1.call-done) | copy-start | bytes 1775620
  674.5 9.3 %collective-permute-start.11 = (bf16[136,1088]{1,0:T(8,128)(2,1)}, bf16[136,1088]{1,0:T(8,128)(2,1)}, u32[]{:S(2)}, u32[]{:S(2)}) collective-permute-start(bf16[136,1088]{1,0:T(8,128)(2,1)} %get-tuple-element.247), channel_id=1, source_target_pairs={{0,16},{16,0},{1,17},{17,1},{2,18},{18,2},{3,19},{19,3},{4,20},{20... | collective-permute-start | bytes 887816 | tf_op jit(solution)/shard_map/ppermute | solution.py:74
  (73 other events, 575.0 us)
Sparse Core Ops, SparseCore 0:
  10.5 46.0 all-gather.18
  58.8 17.4 all-gather.10
  78.4 48.7 all-gather.12
  185.6 38.2 all-reduce.3
  226.0 50.2 all-gather.20
  278.3 15.8 all-gather.16
  297.3 53.5 all-gather.14
  361.1 35.2 all-reduce.5
  413.7 39.9 all-reduce.7
  456.0 24.3 reduce-scatter.15
  483.5 24.4 reduce-scatter.9
  510.4 48.2 reduce-scatter.11
  561.1 56.9 reduce-scatter.13
  620.3 52.4 reduce-scatter.17

commit v2 on v1

--- a/solution.py
+++ b/solution.py
@@ -59,8 +59,115 @@
     return (result, jnp.sum(upstream * centred, axis=0), jnp.sum(upstream, axis=0))
 
 
+def step_right(block, senders):
+    return lax.ppermute(block, "row", [(q, q + 1) for q in senders])
+
+
+def step_left(block, senders):
+    return lax.ppermute(block, "row", [(q, q - 1) for q in senders])
+
+
+def gather_rows(block):
+    count = lax.axis_size("row")
+    mine = lax.axis_index("row")
+    size = block.shape[0]
+    from_left, from_right = [], []
+    lefts, rights = block, block
+    for step in range(1, count):
+        lefts = step_right(lefts, range(step - 1, count - 1))
+        rights = step_left(rights, range(1, count - step + 1))
+        from_left.append(lefts)
+        from_right.append(rights)
+    whole = jnp.zeros((size * count,) + block.shape[1:], block.dtype)
+    whole = lax.dynamic_update_slice_in_dim(whole, block, mine * size, 0)
+    for step in range(1, count):
+        piece = jnp.where(mine >= step, from_left[step - 1], from_right[count - step - 1])
+        place = lax.rem(mine - step + count, count)
+        whole = lax.dynamic_update_slice_in_dim(whole, piece, place * size, 0)
+    return whole
+
+
 def reduce_rows(grad):
-    return lax.psum_scatter(grad, "row", scatter_dimension=0, tiled=True)
+    count = lax.axis_size("row")
+    mine = lax.axis_index("row")
+    size = grad.shape[0] // count
+
+    def own_block(index):
+        return lax.dynamic_slice_in_dim(grad, jnp.clip(index, 0, count - 1) * size, size, 0)
+
+    lefts, rights = None, None
+    for step in range(1, count):
+        up = own_block(mine + count - step)
+        down = own_block(mine - count + step)
+        if lefts is not None:
+            up = (up.astype(jnp.float32) + lefts.astype(jnp.float32)).astype(grad.dtype)
+            down = (down.astype(jnp.float32) + rights.astype(jnp.float32)).astype(grad.dtype)
+        lefts = step_right(up, range(step))
+        rights = step_left(down, range(count - step, count))
+    total = own_block(mine).astype(jnp.float32) + lefts.astype(jnp.float32)
+    return (total + rights.astype(jnp.float32)).astype(grad.dtype)
+
+
+def swap_cols(block, bit):
+    return lax.ppermute(block, "col", [(c, c ^ bit) for c in range(lax.axis_size("col"))])
+
+
+def gather_features(block):
+    mine = lax.axis_index("col")
+    near = swap_cols(block, 1)
+    pair = jnp.stack([block, near])
+    both = jnp.concatenate([pair, swap_cols(pair, 2)], axis=0)
+    return jnp.concatenate(
+        [
+            lax.dynamic_index_in_dim(both, mine ^ j, 0, keepdims=False)
+            for j in range(lax.axis_size("col"))
+        ],
+        axis=1,
+    )
+
+
+def sum_cols(part):
+    half = part.shape[0] // 2
+    side = lax.axis_index("col") % 2
+    wide = jnp.float32
+    kept = lax.dynamic_slice_in_dim(part, side * half, half, 0)
+    sent = lax.dynamic_slice_in_dim(part, (1 - side) * half, half, 0)
+    chip = (kept.astype(wide) + swap_cols(sent, 1).astype(wide)).astype(part.dtype)
+    both = (chip.astype(wide) + swap_cols(chip, 2).astype(wide)).astype(part.dtype)
+    other = swap_cols(both, 1)
+    return jnp.where(
+        side == 0,
+        jnp.concatenate([both, other], axis=0),
+        jnp.concatenate([other, both], axis=0),
+    )
+
+
+def gather_groups(block, dim):
+    count = lax.axis_size("dp")
+    if count != 2:
+        return lax.all_gather(block, "dp", axis=dim, tiled=True)
+    other = lax.ppermute(block, "dp", [(0, 1), (1, 0)])
+    first = lax.axis_index("dp") == 0
+    return jnp.where(
+        first,
+        jnp.concatenate([block, other], axis=dim),
+        jnp.concatenate([other, block], axis=dim),
+    )
+
+
+def with_halo(units, own_start):
+    count = lax.axis_size("col")
+    width = units.shape[-1]
+    from_left = lax.ppermute(
+        units[..., width - HALO :], "col", [(i, i + 1) for i in range(count - 1)]
+    )
+    from_right = lax.ppermute(units[..., :HALO], "col", [(i + 1, i) for i in range(count - 1)])
+    return lax.dynamic_slice_in_dim(
+        jnp.concatenate([from_left, units, from_right], axis=-1),
+        HALO - own_start,
+        EXT,
+        units.ndim - 1,
+    )
 
 
 def reduce_groups(grad, dim):
@@ -130,9 +237,9 @@
     pack_len = block_in.shape[0]
 
     x_part = swap_grid(block_in)
-    x_bf = lax.all_gather(x_part, "col", axis=1, tiled=True)
+    x_bf = gather_features(x_part)
     cot_part = swap_grid(cotangent)
-    cot = lax.all_gather(cot_part, "col", axis=1, tiled=True)
+    cot = gather_features(cot_part)
 
     small = jnp.concatenate(
         [row_vectors.reshape(-1), fc1_bias.reshape(-1), qkv_bias.reshape(-1)]
@@ -154,30 +261,30 @@
 
     ext_start = my_col * (EXT - HD)
     own_start = my_col * (part - (EXT - HD))
-    qkv_cols = lax.all_gather(
-        qkv_weight[:, 0, :].astype(short), ("col", "dp"), axis=1, tiled=True
-    )
-    qkv_ext = jnp.concatenate(
-        [lax.dynamic_slice_in_dim(qkv_cols, i * D + ext_start, EXT, 1) for i in range(3)], axis=1
-    )
-    w_qkv = lax.all_gather(qkv_ext, "row", axis=0, tiled=True)
+    odd = (my_col % 2) == 1
+    qkv_block = gather_groups(qkv_weight[:, 0, :].astype(short), 1)
+    first_unit, unit_b, last_unit = (qkv_block[:, i * part : (i + 1) * part] for i in range(3))
+    arrived = jnp.stack(
+        [
+            jnp.where(odd, last_unit, first_unit),
+            swap_cols(unit_b, 1),
+            swap_cols(jnp.where(odd, first_unit, last_unit), 2),
+        ]
+    )
+    qkv_units = jnp.stack(
+        [
+            lax.dynamic_index_in_dim(arrived, jnp.array(table)[my_col], 0, keepdims=False)
+            for table in ((0, 1, 2, 2), (1, 0, 0, 1), (2, 2, 1, 0))
+        ]
+    )
+    qkv_ext = with_halo(qkv_units, own_start)
+    w_qkv = gather_rows(jnp.concatenate([qkv_ext[0], qkv_ext[1], qkv_ext[2]], axis=1))
     bias_qkv = lax.dynamic_slice_in_dim(bias_qkv_all, ext_start, EXT, 1).reshape(-1)
 
     proj_t = proj_weight[:, 0, :].astype(short).T
-    halo = HALO
-    from_left = lax.ppermute(
-        proj_t[:, part - halo :], "col", [(i, i + 1) for i in range(n_col - 1)]
-    )
-    from_right = lax.ppermute(proj_t[:, :halo], "col", [(i + 1, i) for i in range(n_col - 1)])
-    proj_ext = lax.dynamic_slice_in_dim(
-        jnp.concatenate([from_left, proj_t, from_right], axis=1), halo - own_start, EXT, 1
-    )
-    w_proj_t = lax.all_gather(proj_ext, ("row", "dp"), axis=0, tiled=True)
-    fc1_cols = lax.all_gather(fc1_weight[:, 0, :].astype(short), "dp", axis=1, tiled=True)
-    w_fc1 = lax.all_gather(fc1_cols, "row", axis=0, tiled=True)
-    w_fc2_t = lax.all_gather(
-        fc2_weight[:, 0, :].astype(short).T, ("row", "dp"), axis=0, tiled=True
-    )
+    w_proj_t = gather_rows(gather_groups(with_halo(proj_t, own_start), 0))
+    w_fc1 = gather_rows(gather_groups(fc1_weight[:, 0, :].astype(short), 1))
+    w_fc2_t = gather_rows(gather_groups(fc2_weight[:, 0, :].astype(short).T, 0))
 
     x_full = x_bf.astype(wide)
     mean_one, scale_one = row_stats(x_full)
@@ -204,7 +311,7 @@
     att_own = jnp.where(own[None, :], join_heads(attended), 0).astype(short)
     x_mid = (
         x_full
-        + lax.psum(weigh(att_own, w_proj_t, True).astype(short), "col").astype(wide)
+        + sum_cols(weigh(att_own, w_proj_t, True).astype(short)).astype(wide)
         + vectors[2]
     )
 
@@ -229,7 +336,7 @@
     cot_wide = cot.astype(wide)
     grad_bias_two = jnp.sum(cot_wide, axis=0)
     grad_bias_fc1 = jnp.sum(grad_pre.astype(wide), axis=0)
-    grad_normed_two = lax.psum(weigh(grad_pre, w_fc1, True).astype(short), "col").astype(wide)
+    grad_normed_two = sum_cols(weigh(grad_pre, w_fc1, True).astype(short)).astype(wide)
     back_two, gain_two, shift_two = norm_backward(
         grad_normed_two, centred_two, scale_two, vectors[3]
     )
@@ -263,13 +370,12 @@
         lax.dynamic_index_in_dim(stacked, jnp.array(table)[my_col], 0, keepdims=False)
         for table in ((0, 1, 1, 2), (1, 0, 2, 1), (2, 2, 0, 0))
     ]
-    unit_b = lax.ppermute(picks[1], "col", [(0, 1), (1, 0), (2, 3), (3, 2)])
-    unit_c = lax.ppermute(picks[2], "col", [(0, 2), (2, 0), (1, 3), (3, 1)])
-    odd = (my_col % 2) == 1
+    unit_b = swap_cols(picks[1], 1)
+    unit_c = swap_cols(picks[2], 2)
     grad_block = jnp.concatenate(
         [jnp.where(odd, unit_c, picks[0]), unit_b, jnp.where(odd, picks[0], unit_c)], axis=1
     )
-    grad_normed_one = lax.psum(weigh(grad_ext, w_qkv, True).astype(short), "col").astype(wide)
+    grad_normed_one = sum_cols(weigh(grad_ext, w_qkv, True).astype(short)).astype(wide)
     grad_qkv = outer_sum(normed_one, grad_block).astype(short)
     shard_qkv = reduce_groups(reduce_rows(grad_qkv), 1)
     grad_bias_qkv = jnp.sum(grad_block.astype(wide), axis=0)

time: 720 us -> 667 us (0.926)
  starting transfers between devices: 17.1 us -> 150 us
  waiting for transfers between devices: 321 us -> 190 us
  blocking collectives: 154 us -> 111 us
  local copies, waits for them, and re-layouts: 99.3 us -> 58.8 us
  other arithmetic: 50.8 us -> 86.2 us
  matrix products: 49.1 us -> 31.6 us
  between operations: 21.3 us -> 28.8 us
    all_gather x6 -> x0, waiting for transfers between devices: 164 us -> none  [the longest x1 56.6 us: on_device(): lax.all_gather(fc2_weight[:, 0, :].astype(short).T, ('row', 'dp'), axis=0...]
    ppermute x4 -> x73, waiting for transfers between devices: 8.86 us -> 173 us  [the longest x24 98.8 us: step_left(): return lax.ppermute(block, 'row', [(q, q - 1) for q in senders])]
    ppermute x4 -> x73, starting transfers between devices: 5.34 us -> 141 us  [the longest x24 84.3 us: step_right(): return lax.ppermute(block, 'row', [(q, q + 1) for q in senders])]
    psum x3 -> x0, waiting for transfers between devices: 47.7 us -> none  [the longest x1 34.9 us: on_device(): lax.psum(weigh(grad_pre, w_fc1, True).astype(short), 'col').astype(wide)]
    reduce_scatter x2 -> x0, waiting for transfers between devices: 46.3 us -> none  [reduce_rows(): return lax.psum_scatter(grad, 'row', scatter_dimension=0, tiled=True)]
    unnamed x16 -> x1, waiting for transfers between devices: 46.2 us -> 0.02 us
    all_gather x2 -> x0, blocking collectives: 45.8 us -> none  [the longest x1 32.5 us: on_device(): w_proj_t = lax.all_gather(proj_ext, ('row', 'dp'), axis=0, tiled=True)]
    convert_element_type x0 -> x23, other arithmetic: none -> 29.4 us  [the longest x8 12.7 us: reduce_rows(): up = (up.astype(jnp.float32) + lefts.astype(jnp.float32)).astype(grad.dtype)]
  transfers between devices with their start and end apart: 26 -> 82, of which waited for: 12 -> 26; matrix products, arithmetic and copies ran while one was open for 19% -> 20% of each run, Pallas kernels for 0% -> 0%
where the time goes in v2:
time: 667 us; the launch traced here: 657 us
  waiting for transfers between devices  190 us (28%)
  starting transfers between devices  150 us (22%)
  blocking collectives  111 us (17%)
  other arithmetic  86.2 us (13%)
  local copies, waits for them, and re-layouts  58.8 us (9%)
  matrix products  31.6 us (5%)
  between operations  28.8 us (4%)
    ppermute x24, waiting for transfers between devices, step_left(): return lax.ppermute(block, 'row', [(q, q - 1) for q in senders])  98.8 us
    ppermute x24, starting transfers between devices, step_right(): return lax.ppermute(block, 'row', [(q, q + 1) for q in senders])  84.3 us
    all_gather x1, blocking collectives, on_device(): small_all = lax.all_gather(small, ('row', 'col', 'dp'), axis=0, tiled=False)  68.3 us
    ppermute x24, waiting for transfers between devices, step_right(): return lax.ppermute(block, 'row', [(q, q + 1) for q in senders])  60.3 us
    psum x1, blocking collectives, on_device(): lax.psum(jnp.concatenate([row_grads.reshape(-1), grad_bias_fc1, grad_bias...  42.7 us
    ppermute x24, starting transfers between devices, step_left(): return lax.ppermute(block, 'row', [(q, q - 1) for q in senders])  29.8 us
    unnamed x246, local copies, waits for them, and re-layouts  28.2 us
    dot_general x8, matrix products, weigh(): lax.dot_general(row_block, weight, (((1,), (1 if transposed else 0,)), ((...  18.6 us
  transfers between devices with their start and end apart: 82, of which 26 were waited for; matrix products, arithmetic and copies ran while one was open for 20% of the time, Pallas kernels for 0%

profile of v2, /device:TPU:0, one launch (start us, length us, event | category | flops | bytes accessed | tf_op | source)
XLA Modules:
  0.0 656.9 jit_solution(2344890197387074956)
XLA Ops:
  21.6 68.3 %all-gather = bf16[32,1,1768]{2,1,0:T(2,128)(2,1)S(1)} all-gather(bf16[1,1,1768]{2,1,0:T(2,128)(2,1)S(1)} %bitcast.302), channel_id=1, replica_groups=mesh['dp'=2,'row'=4,'col'=4] {'row','col','dp'}, dimensions={0}, use_global_device_ids=true | all-gather | bytes 116688 | tf_op jit(solution)/shard_map/all_gather | solution.py:249
  127.8 5.2 collective-permute-start.8
  134.6 23.1 %collective-permute-done.20 = bf16[272,320]{1,0:T(8,128)(2,1)S(1)} collective-permute-done((bf16[272,320]{1,0:T(8,128)(2,1)S(1)}, bf16[272,320]{1,0:T(8,128)(2,1)S(1)}, u32[]{:S(2)}, u32[]{:S(2)}) %collective-permute-start.20) | collective-permute-done | bytes 174112 | tf_op jit(solution)/shard_map/ppermute | solution.py:67
  160.3 5.4 collective-permute-start.27
  168.0 5.1 collective-permute-done.2
  179.4 20.1 %collective-permute-done.11 = bf16[272,960]{1,0:T(8,128)(2,1)S(1)} collective-permute-done((bf16[272,960]{1,0:T(8,128)(2,1)S(1)}, bf16[272,960]{1,0:T(8,128)(2,1)S(1)}, u32[]{:S(2)}, u32[]{:S(2)}) %collective-permute-start.11) | collective-permute-done | bytes 522272 | tf_op jit(solution)/shard_map/ppermute | solution.py:67
  218.2 15.5 %collective-permute-done.30 = bf16[272,1088]{1,0:T(8,128)(2,1)S(1)} collective-permute-done((bf16[272,1088]{1,0:T(8,128)(2,1)}, bf16[272,1088]{1,0:T(8,128)(2,1)S(1)}, u32[]{:S(2)}, u32[]{:S(2)}) %collective-permute-start.30) | collective-permute-done | bytes 591904 | tf_op jit(solution)/shard_map/ppermute | solution.py:67
  246.0 4.8 collective-permute-start.74
  252.3 11.6 %collective-permute-done.74 = bf16[272,1088]{1,0:T(8,128)(2,1)} collective-permute-done((bf16[272,1088]{1,0:T(8,128)(2,1)}, bf16[272,1088]{1,0:T(8,128)(2,1)}, u32[]{:S(2)}, u32[]{:S(2)}) %collective-permute-start.74) | collective-permute-done | bytes 591904 | tf_op jit(solution)/shard_map/ppermute | solution.py:63
  266.2 5.2 collective-permute-start.75
  271.4 12.3 %collective-permute-done.75 = bf16[272,1088]{1,0:T(8,128)(2,1)} collective-permute-done((bf16[272,1088]{1,0:T(8,128)(2,1)}, bf16[272,1088]{1,0:T(8,128)(2,1)}, u32[]{:S(2)}, u32[]{:S(2)}) %collective-permute-start.75) | collective-permute-done | bytes 591904 | tf_op jit(solution)/shard_map/ppermute | solution.py:63
  288.2 5.0 collective-permute-start.76
  296.8 7.8 %collective-permute-done.76 = bf16[272,1088]{1,0:T(8,128)(2,1)} collective-permute-done((bf16[272,1088]{1,0:T(8,128)(2,1)}, bf16[272,1088]{1,0:T(8,128)(2,1)}, u32[]{:S(2)}, u32[]{:S(2)}) %collective-permute-start.76) | collective-permute-done | bytes 591904 | tf_op jit(solution)/shard_map/ppermute | solution.py:63
  304.6 17.4 %collective-permute-done.79 = bf16[272,1088]{1,0:T(8,128)(2,1)} collective-permute-done((bf16[272,1088]{1,0:T(8,128)(2,1)}, bf16[272,1088]{1,0:T(8,128)(2,1)}, u32[]{:S(2)}, u32[]{:S(2)}) %collective-permute-start.79) | collective-permute-done | bytes 591904 | tf_op jit(solution)/shard_map/ppermute | solution.py:67
  325.7 6.7 %collective-permute-done.80 = bf16[136,1088]{1,0:T(8,128)(2,1)} collective-permute-done((bf16[136,1088]{1,0:T(8,128)(2,1)}, bf16[136,1088]{1,0:T(8,128)(2,1)}, u32[]{:S(2)}, u32[]{:S(2)}) %collective-permute-start.80) | collective-permute-done | bytes 295968 | tf_op jit(solution)/shard_map/ppermute | solution.py:181
  336.3 6.4 collective-permute-done.33
  348.8 5.4 collective-permute-start.34
  354.2 5.7 collective-permute-done.35
  388.3 11.3 %collective-permute-done.37 = bf16[272,1088]{1,0:T(8,128)(2,1)S(1)} collective-permute-done((bf16[272,1088]{1,0:T(8,128)(2,1)}, bf16[272,1088]{1,0:T(8,128)(2,1)S(1)}, u32[]{:S(2)}, u32[]{:S(2)}) %collective-permute-start.37) | collective-permute-done | bytes 591904 | tf_op jit(solution)/shard_map/ppermute | solution.py:67
  405.1 6.1 convert_reduce_fusion.4
  424.0 8.4 %collective-permute-done.67 = bf16[272,1088]{1,0:T(8,128)(2,1)S(1)} collective-permute-done((bf16[272,1088]{1,0:T(8,128)(2,1)S(1)}, bf16[272,1088]{1,0:T(8,128)(2,1)S(1)}, u32[]{:S(2)}, u32[]{:S(2)}) %collective-permute-start.67) | collective-permute-done | bytes 591904 | tf_op jit(solution)/shard_map/ppermute | solution.py:63
  433.3 5.2 collective-permute-start.68
  444.5 6.6 %collective-permute-done.68 = bf16[272,1088]{1,0:T(8,128)(2,1)} collective-permute-done((bf16[272,1088]{1,0:T(8,128)(2,1)}, bf16[272,1088]{1,0:T(8,128)(2,1)}, u32[]{:S(2)}, u32[]{:S(2)}) %collective-permute-start.68) | collective-permute-done | bytes 591904 | tf_op jit(solution)/shard_map/ppermute | solution.py:63
  454.7 6.2 collective-permute-start.69
  488.0 5.0 collective-permute-start.61
  498.8 6.0 collective-permute-start.53
  505.6 7.2 %collective-permute-start.62 = (bf16[272,272]{0,1:T(8,128)(2,1)S(1)}, bf16[272,272]{0,1:T(8,128)(2,1)S(1)}, u32[]{:S(2)}, u32[]{:S(2)}) collective-permute-start(bf16[272,272]{0,1:T(8,128)(2,1)S(1)} %get-tuple-element.244), channel_id=1, source_target_pairs={{0,4},{4,8},{8,12},{1,5},{5,9},{9,13},{2,6},{6,10},{10,14},{3,7},{... | collective-permute-start | bytes 443912 | tf_op jit(solution)/shard_map/ppermute | solution.py:63
  552.8 6.8 %collective-permute-done.54 = bf16[272,816]{1,0:T(8,128)(2,1)S(1)} collective-permute-done((bf16[272,816]{1,0:T(8,128)(2,1)S(1)}, bf16[272,816]{1,0:T(8,128)(2,1)S(1)}, u32[]{:S(2)}, u32[]{:S(2)}) %collective-permute-start.54) | collective-permute-done | bytes 443936 | tf_op jit(solution)/shard_map/ppermute | solution.py:63
  567.5 5.0 collective-permute-start.55
  576.5 42.7 %psum.7 = f32[8432]{0:T(1024)S(1)} all-reduce(f32[8432]{0:T(1024)S(1)} %concatenate.112), channel_id=1, replica_groups=mesh['dp'=2,'row'=4,'col'=4] {'row','dp'}, use_global_device_ids=true, to_apply=%region_22.23 | all-reduce | flops 8432 | bytes 67456 | tf_op jit(solution)/shard_map/psum | solution.py:391
  622.1 4.7 fusion.76
  635.1 7.2 %collective-permute-done.59 = bf16[272,408]{1,0:T(8,128)(2,1)S(1)} collective-permute-done((bf16[272,408]{1,0:T(8,128)(2,1)S(1)}, bf16[272,408]{1,0:T(8,128)(2,1)S(1)}, u32[]{:S(2)}, u32[]{:S(2)}) %collective-permute-start.59) | collective-permute-done | bytes 221984 | tf_op jit(solution)/shard_map/ppermute | solution.py:181
  (580 shorter events, 268.5 us)
Async XLA Ops:
  7.2 514.9 %reduce-scatter.2.cloned.1.call-start = ((), (), s32[]{:S(2)}) async-start(), calls=%async_computation.1 | async-start | bytes 1392640 | tf_op jit(solution)/shard_map/reduce_scatter | solution.py:323
  8.8 83.7 %collective-permute-start.3 = (bf16[272,408]{1,0:T(8,128)(2,1)S(1)}, bf16[272,408]{1,0:T(8,128)(2,1)S(1)}, u32[]{:S(2)}, u32[]{:S(2)}) collective-permute-start(bf16[272,408]{1,0:T(8,128)(2,1)S(1)} %bitcast.295), channel_id=1, source_target_pairs={{0,16},{16,0},{1,17},{17,1},{2,18},{18,2},{3,19},{19,3},{4,20},{20... | collective-permute-start | bytes 665864 | tf_op jit(solution)/shard_map/ppermute | solution.py:149
  11.8 102.4 %collective-permute-start = (bf16[512,272]{0,1:T(8,128)(2,1)}, bf16[512,272]{0,1:T(8,128)(2,1)S(1)}, u32[]{:S(2)}, u32[]{:S(2)}) collective-permute-start(bf16[512,272]{0,1:T(8,128)(2,1)} %param.23), channel_id=1, source_target_pairs={{0,0},{1,4},{2,8},{3,12},{4,1},{5,5},{6,9},{7,13},{8,2},{9,6},{10,... | collective-permute-start | bytes 835592 | tf_op jit(solution)/shard_map/ppermute | solution.py:45
  14.4 77.7 %collective-permute-start.14 = (bf16[136,48]{1,0:T(8,128)(2,1)S(1)}, bf16[136,48]{1,0:T(8,128)(2,1)S(1)}, u32[]{:S(2)}, u32[]{:S(2)}) collective-permute-start(bf16[136,48]{1,0:T(8,128)(2,1)S(1)} %get-tuple-element.265), channel_id=1, source_target_pairs={{0,1},{1,2},{2,3},{4,5},{5,6},{6,7},{8,9},{9,10},{10,11},{12,13},{... | collective-permute-start | bytes 39176 | tf_op jit(solution)/shard_map/ppermute | solution.py:161
  18.4 73.8 %collective-permute-start.15 = (bf16[136,48]{1,0:T(8,128)(2,1)S(1)}, bf16[136,48]{1,0:T(8,128)(2,1)S(1)}, u32[]{:S(2)}, u32[]{:S(2)}) collective-permute-start(bf16[136,48]{1,0:T(8,128)(2,1)S(1)} %get-tuple-element.266), channel_id=1, source_target_pairs={{1,0},{2,1},{3,2},{5,4},{6,5},{7,6},{9,8},{10,9},{11,10},{13,12},{... | collective-permute-start | bytes 39176 | tf_op jit(solution)/shard_map/ppermute | solution.py:164
  19.7 95.9 %collective-permute-start.41 = (bf16[512,272]{0,1:T(8,128)(2,1)}, bf16[512,272]{0,1:T(8,128)(2,1)S(1)}, u32[]{:S(2)}, u32[]{:S(2)}) collective-permute-start(bf16[512,272]{0,1:T(8,128)(2,1)} %param.24), channel_id=1, source_target_pairs={{0,0},{1,4},{2,8},{3,12},{4,1},{5,5},{6,9},{7,13},{8,2},{9,6},{10,... | collective-permute-start | bytes 835592 | tf_op jit(solution)/shard_map/ppermute | solution.py:45
  122.4 36.4 %collective-permute-start.9 = (bf16[272,960]{1,0:T(8,128)(2,1)S(1)}, bf16[272,960]{1,0:T(8,128)(2,1)S(1)}, u32[]{:S(2)}, u32[]{:S(2)}) collective-permute-start(bf16[272,960]{1,0:T(8,128)(2,1)S(1)} %get-tuple-element.194), channel_id=1, source_target_pairs={{4,0},{8,4},{12,8},{5,1},{9,5},{13,9},{6,2},{10,6},{14,10},{7,3},{... | collective-permute-start | bytes 1566728 | tf_op jit(solution)/shard_map/ppermute | solution.py:67
  125.1 40.6 %collective-permute-start.28 = (bf16[272,1088]{1,0:T(8,128)(2,1)}, bf16[272,1088]{1,0:T(8,128)(2,1)S(1)}, u32[]{:S(2)}, u32[]{:S(2)}) collective-permute-start(bf16[272,1088]{1,0:T(8,128)(2,1)} %get-tuple-element.198), channel_id=1, source_target_pairs={{4,0},{8,4},{12,8},{5,1},{9,5},{13,9},{6,2},{10,6},{14,10},{7,3},{... | collective-permute-start | bytes 1775624 | tf_op jit(solution)/shard_map/ppermute | solution.py:67
  126.4 31.2 %collective-permute-start.20 = (bf16[272,320]{1,0:T(8,128)(2,1)S(1)}, bf16[272,320]{1,0:T(8,128)(2,1)S(1)}, u32[]{:S(2)}, u32[]{:S(2)}) collective-permute-start(bf16[272,320]{1,0:T(8,128)(2,1)S(1)} %collective-permute-done.19), channel_id=1, source_target_pairs={{4,0},{5,1},{6,2},{7,3},{20,16},{21,17},{22,18},{23,19}} | collective-permute-start | bytes 522248 | tf_op jit(solution)/shard_map/ppermute | solution.py:67
  127.8 38.9 %collective-permute-start.8 = (bf16[272,960]{1,0:T(8,128)(2,1)S(1)}, bf16[272,960]{1,0:T(8,128)(2,1)S(1)}, u32[]{:S(2)}, u32[]{:S(2)}) collective-permute-start(bf16[272,960]{1,0:T(8,128)(2,1)S(1)} %get-tuple-element.194), channel_id=1, source_target_pairs={{0,4},{4,8},{8,12},{1,5},{5,9},{9,13},{2,6},{6,10},{10,14},{3,7},{... | collective-permute-start | bytes 1566728 | tf_op jit(solution)/shard_map/ppermute | solution.py:63
  133.0 27.2 %collective-permute-start.22 = (bf16[272,320]{1,0:T(8,128)(2,1)S(1)}, bf16[272,320]{1,0:T(8,128)(2,1)S(1)}, u32[]{:S(2)}, u32[]{:S(2)}) collective-permute-start(bf16[272,320]{1,0:T(8,128)(2,1)S(1)} %collective-permute-done.21), channel_id=1, source_target_pairs={{8,12},{9,13},{10,14},{11,15},{24,28},{25,29},{26,30},{27,31}} | collective-permute-start | bytes 522248 | tf_op jit(solution)/shard_map/ppermute | solution.py:63
  160.3 50.6 %collective-permute-start.27 = (bf16[272,1088]{1,0:T(8,128)(2,1)}, bf16[272,1088]{1,0:T(8,128)(2,1)}, u32[]{:S(2)}, u32[]{:S(2)}) collective-permute-start(bf16[272,1088]{1,0:T(8,128)(2,1)} %get-tuple-element.198), channel_id=1, source_target_pairs={{0,4},{4,8},{8,12},{1,5},{5,9},{9,13},{2,6},{6,10},{10,14},{3,7},{... | collective-permute-start | bytes 1775624 | tf_op jit(solution)/shard_map/ppermute | solution.py:63
  165.8 45.8 %collective-permute-start.43 = (bf16[2,512,272]{1,2,0:T(8,128)(2,1)}, bf16[2,512,272]{1,2,0:T(8,128)(2,1)}, u32[]{:S(2)}, u32[]{:S(2)}) collective-permute-start(bf16[2,512,272]{1,2,0:T(8,128)(2,1)} %pad_maximum_fusion.12), channel_id=1, source_target_pairs={{0,2},{1,3},{2,0},{3,1},{4,6},{5,7},{6,4},{7,5},{8,10},{9,11},{10,... | collective-permute-start | bytes 1671176 | tf_op jit(solution)/shard_map/ppermute | solution.py:112
  166.7 46.0 %collective-permute-start.29 = (bf16[272,1088]{1,0:T(8,128)(2,1)S(1)}, bf16[272,1088]{1,0:T(8,128)(2,1)}, u32[]{:S(2)}, u32[]{:S(2)}) collective-permute-start(bf16[272,1088]{1,0:T(8,128)(2,1)S(1)} %collective-permute-done.28), channel_id=1, source_target_pairs={{4,0},{8,4},{5,1},{9,5},{6,2},{10,6},{7,3},{11,7},{20,16},{24,20},... | collective-permute-start | bytes 1775624 | tf_op jit(solution)/shard_map/ppermute | solution.py:67
  176.3 23.3 %collective-permute-start.11 = (bf16[272,960]{1,0:T(8,128)(2,1)S(1)}, bf16[272,960]{1,0:T(8,128)(2,1)S(1)}, u32[]{:S(2)}, u32[]{:S(2)}) collective-permute-start(bf16[272,960]{1,0:T(8,128)(2,1)S(1)} %collective-permute-done.10), channel_id=1, source_target_pairs={{4,0},{5,1},{6,2},{7,3},{20,16},{21,17},{22,18},{23,19}} | collective-permute-start | bytes 1566728 | tf_op jit(solution)/shard_map/ppermute | solution.py:67
  178.2 21.8 %collective-permute-start.13 = (bf16[272,960]{1,0:T(8,128)(2,1)S(1)}, bf16[272,960]{1,0:T(8,128)(2,1)S(1)}, u32[]{:S(2)}, u32[]{:S(2)}) collective-permute-start(bf16[272,960]{1,0:T(8,128)(2,1)S(1)} %collective-permute-done.12), channel_id=1, source_target_pairs={{8,12},{9,13},{10,14},{11,15},{24,28},{25,29},{26,30},{27,31}} | collective-permute-start | bytes 1566728 | tf_op jit(solution)/shard_map/ppermute | solution.py:63
  212.8 20.9 %collective-permute-start.30 = (bf16[272,1088]{1,0:T(8,128)(2,1)}, bf16[272,1088]{1,0:T(8,128)(2,1)S(1)}, u32[]{:S(2)}, u32[]{:S(2)}) collective-permute-start(bf16[272,1088]{1,0:T(8,128)(2,1)} %collective-permute-done.29), channel_id=1, source_target_pairs={{4,0},{5,1},{6,2},{7,3},{20,16},{21,17},{22,18},{23,19}} | collective-permute-start | bytes 1775624 | tf_op jit(solution)/shard_map/ppermute | solution.py:67
  250.8 20.6 %collective-permute-start.77 = (bf16[272,1088]{1,0:T(8,128)(2,1)}, bf16[272,1088]{1,0:T(8,128)(2,1)}, u32[]{:S(2)}, u32[]{:S(2)}) collective-permute-start(bf16[272,1088]{1,0:T(8,128)(2,1)} %get-tuple-element.204), channel_id=1, source_target_pairs={{12,8},{13,9},{14,10},{15,11},{28,24},{29,25},{30,26},{31,27}} | collective-permute-start | bytes 1775624 | tf_op jit(solution)/shard_map/ppermute | solution.py:67
  295.5 26.5 %collective-permute-start.79 = (bf16[272,1088]{1,0:T(8,128)(2,1)}, bf16[272,1088]{1,0:T(8,128)(2,1)}, u32[]{:S(2)}, u32[]{:S(2)}) collective-permute-start(bf16[272,1088]{1,0:T(8,128)(2,1)} %add_convert_fusion.4), channel_id=1, source_target_pairs={{4,0},{8,4},{12,8},{5,1},{9,5},{13,9},{6,2},{10,6},{14,10},{7,3},{... | collective-permute-start | bytes 1775624 | tf_op jit(solution)/shard_map/ppermute | solution.py:67
  348.8 33.6 %collective-permute-start.34 = (bf16[272,1088]{1,0:T(8,128)(2,1)}, bf16[272,1088]{1,0:T(8,128)(2,1)}, u32[]{:S(2)}, u32[]{:S(2)}) collective-permute-start(bf16[272,1088]{1,0:T(8,128)(2,1)} %get-tuple-element.200), channel_id=1, source_target_pairs={{0,4},{4,8},{8,12},{1,5},{5,9},{9,13},{2,6},{6,10},{10,14},{3,7},{... | collective-permute-start | bytes 1775624 | tf_op jit(solution)/shard_map/ppermute | solution.py:63
  359.9 23.2 %collective-permute-start.36 = (bf16[272,1088]{1,0:T(8,128)(2,1)}, bf16[272,1088]{1,0:T(8,128)(2,1)}, u32[]{:S(2)}, u32[]{:S(2)}) collective-permute-start(bf16[272,1088]{1,0:T(8,128)(2,1)} %collective-permute-done.35), channel_id=1, source_target_pairs={{4,0},{8,4},{5,1},{9,5},{6,2},{10,6},{7,3},{11,7},{20,16},{24,20},... | collective-permute-start | bytes 1775624 | tf_op jit(solution)/shard_map/ppermute | solution.py:67
  419.8 24.7 %collective-permute-start.70 = (bf16[272,1088]{1,0:T(8,128)(2,1)}, bf16[272,1088]{1,0:T(8,128)(2,1)}, u32[]{:S(2)}, u32[]{:S(2)}) collective-permute-start(bf16[272,1088]{1,0:T(8,128)(2,1)} %get-tuple-element.208), channel_id=1, source_target_pairs={{12,8},{13,9},{14,10},{15,11},{28,24},{29,25},{30,26},{31,27}} | collective-permute-start | bytes 1775624 | tf_op jit(solution)/shard_map/ppermute | solution.py:67
  422.3 20.8 %collective-permute-start.45 = (bf16[256,1088]{0,1:T(8,128)(2,1)}, bf16[256,1088]{0,1:T(8,128)(2,1)}, u32[]{:S(2)}, u32[]{:S(2)}) collective-permute-start(bf16[256,1088]{0,1:T(8,128)(2,1)} %add_convert_fusion.16), channel_id=1, source_target_pairs={{0,2},{1,3},{2,0},{3,1},{4,6},{5,7},{6,4},{7,5},{8,10},{9,11},{10,... | collective-permute-start | bytes 1671176 | tf_op jit(solution)/shard_map/ppermute | solution.py:112
  453.9 23.6 %collective-permute-start.71 = (bf16[272,1088]{1,0:T(8,128)(2,1)S(1)}, bf16[272,1088]{1,0:T(8,128)(2,1)S(1)}, u32[]{:S(2)}, u32[]{:S(2)}) collective-permute-start(bf16[272,1088]{1,0:T(8,128)(2,1)S(1)} %get-tuple-element.206), channel_id=1, source_target_pairs={{8,4},{12,8},{9,5},{13,9},{10,6},{14,10},{11,7},{15,11},{24,20},{2... | collective-permute-start | bytes 1775624 | tf_op jit(solution)/shard_map/ppermute | solution.py:67
  454.7 79.0 %collective-permute-start.69 = (bf16[272,1088]{1,0:T(8,128)(2,1)}, bf16[272,1088]{1,0:T(8,128)(2,1)}, u32[]{:S(2)}, u32[]{:S(2)}) collective-permute-start(bf16[272,1088]{1,0:T(8,128)(2,1)} %get-tuple-element.205), channel_id=1, source_target_pairs={{0,4},{4,8},{8,12},{1,5},{5,9},{9,13},{2,6},{6,10},{10,14},{3,7},{... | collective-permute-start | bytes 1775624 | tf_op jit(solution)/shard_map/ppermute | solution.py:63
  473.6 39.5 %collective-permute-start.47 = (bf16[256,1088]{0,1:T(8,128)(2,1)S(1)}, bf16[256,1088]{0,1:T(8,128)(2,1)S(1)}, u32[]{:S(2)}, u32[]{:S(2)}) collective-permute-start(bf16[256,1088]{0,1:T(8,128)(2,1)S(1)} %constant_dynamic-slice_fusion.11), channel_id=1, source_target_pairs={{0,1},{1,0},{2,3},{3,2},{4,5},{5,4},{6,7},{7,6},{8,9},{9,8},{10,11... | collective-permute-start | bytes 1671176 | tf_op jit(solution)/shard_map/ppermute | solution.py:112
  486.7 50.7 %collective-permute-start.72 = (bf16[272,1088]{1,0:T(8,128)(2,1)}, bf16[272,1088]{1,0:T(8,128)(2,1)}, u32[]{:S(2)}, u32[]{:S(2)}) collective-permute-start(bf16[272,1088]{1,0:T(8,128)(2,1)} %add_convert_fusion.9), channel_id=1, source_target_pairs={{4,0},{8,4},{12,8},{5,1},{9,5},{13,9},{6,2},{10,6},{14,10},{7,3},{... | collective-permute-start | bytes 1775624 | tf_op jit(solution)/shard_map/ppermute | solution.py:67
  498.8 48.1 %collective-permute-start.53 = (bf16[272,816]{1,0:T(8,128)(2,1)}, bf16[272,816]{1,0:T(8,128)(2,1)}, u32[]{:S(2)}, u32[]{:S(2)}) collective-permute-start(bf16[272,816]{1,0:T(8,128)(2,1)} %get-tuple-element.213), channel_id=1, source_target_pairs={{0,4},{1,5},{2,6},{3,7},{16,20},{17,21},{18,22},{19,23}} | collective-permute-start | bytes 1331720 | tf_op jit(solution)/shard_map/ppermute | solution.py:63
  517.4 35.4 %collective-permute-start.56 = (bf16[272,816]{1,0:T(8,128)(2,1)}, bf16[272,816]{1,0:T(8,128)(2,1)}, u32[]{:S(2)}, u32[]{:S(2)}) collective-permute-start(bf16[272,816]{1,0:T(8,128)(2,1)} %get-tuple-element.214), channel_id=1, source_target_pairs={{12,8},{13,9},{14,10},{15,11},{28,24},{29,25},{30,26},{31,27}} | collective-permute-start | bytes 1331720 | tf_op jit(solution)/shard_map/ppermute | solution.py:67
  527.1 35.3 %collective-permute-start.48 = (bf16[256,1088]{0,1:T(8,128)(2,1)}, bf16[256,1088]{0,1:T(8,128)(2,1)}, u32[]{:S(2)}, u32[]{:S(2)}) collective-permute-start(bf16[256,1088]{0,1:T(8,128)(2,1)} %add_convert_fusion.14), channel_id=1, source_target_pairs={{0,2},{1,3},{2,0},{3,1},{4,6},{5,7},{6,4},{7,5},{8,10},{9,11},{10,... | collective-permute-start | bytes 1671176 | tf_op jit(solution)/shard_map/ppermute | solution.py:112
  567.5 64.6 %collective-permute-start.55 = (bf16[272,816]{1,0:T(8,128)(2,1)}, bf16[272,816]{1,0:T(8,128)(2,1)S(1)}, u32[]{:S(2)}, u32[]{:S(2)}) collective-permute-start(bf16[272,816]{1,0:T(8,128)(2,1)} %get-tuple-element.211), channel_id=1, source_target_pairs={{0,4},{4,8},{8,12},{1,5},{5,9},{9,13},{2,6},{6,10},{10,14},{3,7},{... | collective-permute-start | bytes 1331720 | tf_op jit(solution)/shard_map/ppermute | solution.py:63
  572.8 59.4 %collective-permute-start.58 = (bf16[272,816]{1,0:T(8,128)(2,1)S(1)}, bf16[272,816]{1,0:T(8,128)(2,1)S(1)}, u32[]{:S(2)}, u32[]{:S(2)}) collective-permute-start(bf16[272,816]{1,0:T(8,128)(2,1)S(1)} %add_convert_fusion.20), channel_id=1, source_target_pairs={{4,0},{8,4},{12,8},{5,1},{9,5},{13,9},{6,2},{10,6},{14,10},{7,3},{... | collective-permute-start | bytes 1331720 | tf_op jit(solution)/shard_map/ppermute | solution.py:67
  (165 other events, 2507.7 us)
Sparse Core Ops, SparseCore 0:
  443.2 23.3 reduce-scatter.1

commit v3 on v2

--- a/solution.py
+++ b/solution.py
@@ -87,13 +87,16 @@
     return whole
 
 
-def reduce_rows(grad):
+def reduce_rows(grad, extra=None):
     count = lax.axis_size("row")
     mine = lax.axis_index("row")
     size = grad.shape[0] // count
 
     def own_block(index):
-        return lax.dynamic_slice_in_dim(grad, jnp.clip(index, 0, count - 1) * size, size, 0)
+        block = lax.dynamic_slice_in_dim(grad, jnp.clip(index, 0, count - 1) * size, size, 0)
+        if extra is None:
+            return block
+        return jnp.concatenate([block, extra, pad_rows(extra)], axis=0)
 
     lefts, rights = None, None
     for step in range(1, count):
@@ -153,6 +156,10 @@
         jnp.concatenate([block, other], axis=dim),
         jnp.concatenate([other, block], axis=dim),
     )
+
+
+def pad_rows(row):
+    return jnp.zeros((15,) + row.shape[1:], row.dtype)
 
 
 def with_halo(units, own_start):
@@ -228,9 +235,6 @@
     wide = jnp.float32
     short = jnp.bfloat16
     my_col = lax.axis_index("col")
-    my_row = lax.axis_index("row")
-    my_dp = lax.axis_index("dp")
-    n_dp = lax.axis_size("dp")
     n_col = lax.axis_size("col")
     n_row = lax.axis_size("row")
     part = D // n_col
@@ -241,28 +245,12 @@
     cot_part = swap_grid(cotangent)
     cot = gather_features(cot_part)
 
-    small = jnp.concatenate(
-        [row_vectors.reshape(-1), fc1_bias.reshape(-1), qkv_bias.reshape(-1)]
-    ).astype(short)
-    rv_size = row_vectors.size
-    b1_size = fc1_bias.size
-    small_all = lax.all_gather(small, ("row", "col", "dp"), axis=0, tiled=False)
-    small_all = small_all.reshape(n_row, n_col, n_dp, small.shape[0]).astype(wide)
-    vectors = (
-        small_all[:, 0, :, :rv_size]
-        .reshape(n_row, n_dp, 6, part // n_dp)
-        .transpose(2, 0, 1, 3)
-        .reshape(6, D)
-    )
-    bias_fc1 = lax.dynamic_index_in_dim(
-        small_all[0, :, :, rv_size : rv_size + b1_size], my_col, 0, keepdims=False
-    ).reshape(-1)
-    bias_qkv_all = small_all[0, :, :, rv_size + b1_size :].reshape(3, D)
-
-    ext_start = my_col * (EXT - HD)
     own_start = my_col * (part - (EXT - HD))
     odd = (my_col % 2) == 1
-    qkv_block = gather_groups(qkv_weight[:, 0, :].astype(short), 1)
+    qkv_block = gather_groups(
+        jnp.concatenate([qkv_weight[:, 0, :], qkv_bias, pad_rows(qkv_bias)], axis=0).astype(short),
+        1,
+    )
     first_unit, unit_b, last_unit = (qkv_block[:, i * part : (i + 1) * part] for i in range(3))
     arrived = jnp.stack(
         [
@@ -278,12 +266,27 @@
         ]
     )
     qkv_ext = with_halo(qkv_units, own_start)
-    w_qkv = gather_rows(jnp.concatenate([qkv_ext[0], qkv_ext[1], qkv_ext[2]], axis=1))
-    bias_qkv = lax.dynamic_slice_in_dim(bias_qkv_all, ext_start, EXT, 1).reshape(-1)
+    bias_qkv = qkv_ext[:, part, :].reshape(-1).astype(wide)
+    w_qkv = gather_rows(
+        jnp.concatenate([qkv_ext[0, :part], qkv_ext[1, :part], qkv_ext[2, :part]], axis=1)
+    )
 
     proj_t = proj_weight[:, 0, :].astype(short).T
-    w_proj_t = gather_rows(gather_groups(with_halo(proj_t, own_start), 0))
-    w_fc1 = gather_rows(gather_groups(fc1_weight[:, 0, :].astype(short), 1))
+    vectors_t = row_vectors[:, 0, :].astype(short).T
+    filler = jnp.zeros((vectors_t.shape[0], 384 - EXT - vectors_t.shape[1]), short)
+    proj_all = gather_rows(
+        gather_groups(
+            jnp.concatenate([with_halo(proj_t, own_start), vectors_t, filler], axis=1), 0
+        )
+    )
+    w_proj_t = proj_all[:, :EXT]
+    vectors = proj_all[:, EXT : EXT + 6].astype(wide).T
+    fc1_block = gather_groups(
+        jnp.concatenate([fc1_weight[:, 0, :], fc1_bias, pad_rows(fc1_bias)], axis=0).astype(short),
+        1,
+    )
+    bias_fc1 = fc1_block[part].astype(wide)
+    w_fc1 = gather_rows(fc1_block[:part])
     w_fc2_t = gather_rows(gather_groups(fc2_weight[:, 0, :].astype(short).T, 0))
 
     x_full = x_bf.astype(wide)
@@ -332,10 +335,10 @@
     grad_fc2_t = outer_sum(cot, hidden).astype(short)
     shard_fc2 = reduce_groups(reduce_rows(grad_fc2_t), 0)
     grad_fc1 = outer_sum(normed_two, grad_pre).astype(short)
-    shard_fc1 = reduce_groups(reduce_rows(grad_fc1), 1)
     cot_wide = cot.astype(wide)
     grad_bias_two = jnp.sum(cot_wide, axis=0)
     grad_bias_fc1 = jnp.sum(grad_pre.astype(wide), axis=0)
+    shard_fc1 = reduce_groups(reduce_rows(grad_fc1, grad_bias_fc1[None, :].astype(short)), 1)
     grad_normed_two = sum_cols(weigh(grad_pre, w_fc1, True).astype(short)).astype(wide)
     back_two, gain_two, shift_two = norm_backward(
         grad_normed_two, centred_two, scale_two, vectors[3]
@@ -377,37 +380,27 @@
     )
     grad_normed_one = sum_cols(weigh(grad_ext, w_qkv, True).astype(short)).astype(wide)
     grad_qkv = outer_sum(normed_one, grad_block).astype(short)
-    shard_qkv = reduce_groups(reduce_rows(grad_qkv), 1)
     grad_bias_qkv = jnp.sum(grad_block.astype(wide), axis=0)
+    shard_qkv = reduce_groups(reduce_rows(grad_qkv, grad_bias_qkv[None, :].astype(short)), 1)
     back_one, gain_one, shift_one = norm_backward(
         grad_normed_one, centred_one, scale_one, vectors[0]
     )
     in_grad = lax.dynamic_slice_in_dim(grad_mid + back_one, my_col * part, part, 1)
     block_in_grad = swap_grid(in_grad.astype(short)).astype(wide)
 
+    nothing = jnp.zeros_like(gain_one)
     row_grads = jnp.stack(
-        [gain_one, shift_one, grad_bias_proj, gain_two, shift_two, grad_bias_two]
-    )
-    sums = lax.psum(
-        jnp.concatenate([row_grads.reshape(-1), grad_bias_fc1, grad_bias_qkv]), ("row", "dp")
-    )
-    vec_size = part // n_dp
-    row_shard = lax.dynamic_slice_in_dim(
-        sums[: 6 * D].reshape(6, D), my_row * part + my_dp * vec_size, vec_size, 1
-    )[:, None, :]
-    fc1_bias_shard = lax.dynamic_slice_in_dim(
-        sums[6 * D : 6 * D + grad_bias_fc1.shape[0]], my_dp * b1_size, b1_size, 0
-    )[None, :]
-    qkv_bias_shard = lax.dynamic_slice_in_dim(
-        sums[6 * D + grad_bias_fc1.shape[0] :], my_dp * qkv_bias.size, qkv_bias.size, 0
-    )[None, :]
+        [gain_one, shift_one, grad_bias_proj, gain_two, shift_two, grad_bias_two, nothing, nothing]
+    )
+    row_blocks = row_grads.reshape(8, n_row, part).transpose(1, 0, 2).reshape(8 * n_row, part)
+    row_shard = reduce_groups(reduce_rows(row_blocks), 1)[:6, None, :].astype(wide)
     grads = (
-        shard_qkv.astype(wide)[:, None, :],
+        shard_qkv.astype(wide)[:part, None, :],
         shard_proj.astype(wide).T[:, None, :],
-        shard_fc1.astype(wide)[:, None, :],
+        shard_fc1.astype(wide)[:part, None, :],
         shard_fc2.astype(wide).T[:, None, :],
-        qkv_bias_shard,
-        fc1_bias_shard,
+        shard_qkv.astype(wide)[part : part + 1],
+        shard_fc1.astype(wide)[part : part + 1],
         row_shard,
     )
     masters = (qkv_weight, proj_weight, fc1_weight, fc2_weight, qkv_bias, fc1_bias, row_vectors)

time: 667 us -> 626 us (0.939)
  the two profiles are of different devices: /device:TPU:0 before, /device:TPU:20 now
where the time goes in v3:
time: 626 us; the launch traced here: 614 us
  waiting for transfers between devices  197 us (31%)
  starting transfers between devices  177 us (28%)
  other arithmetic  100 us (16%)
  local copies, waits for them, and re-layouts  80.2 us (13%)
  matrix products  31 us (5%)
  between operations  29.1 us (5%)
    ppermute x27, waiting for transfers between devices, step_right(): return lax.ppermute(block, 'row', [(q, q + 1) for q in senders])  95.9 us
    ppermute x27, waiting for transfers between devices, step_left(): return lax.ppermute(block, 'row', [(q, q - 1) for q in senders])  77.3 us
    ppermute x27, starting transfers between devices, step_left(): return lax.ppermute(block, 'row', [(q, q - 1) for q in senders])  71.5 us
    ppermute x27, starting transfers between devices, step_right(): return lax.ppermute(block, 'row', [(q, q + 1) for q in senders])  65 us
    unnamed x252, local copies, waits for them, and re-layouts  29.2 us
    dot_general x8, matrix products, weigh(): lax.dot_general(row_block, weight, (((1,), (1 if transposed else 0,)), ((...  18 us
    convert_element_type x8, other arithmetic, reduce_rows(): up = (up.astype(jnp.float32) + lefts.astype(jnp.float32)).astype(grad.dtype)  16.7 us
    ppermute x5, waiting for transfers between devices, reduce_groups(): lax.ppermute(sent, 'dp', [(0, 1), (1, 0)]).astype(jnp.float32)  12.7 us
  transfers between devices with their start and end apart: 89, of which 28 were waited for; matrix products, arithmetic and copies ran while one was open for 27% of the time, Pallas kernels for 0%

profile of v3, /device:TPU:20, one launch (start us, length us, event | category | flops | bytes accessed | tf_op | source)
XLA Modules:
  0.0 614.1 jit_solution(11095310996841907912)
XLA Ops:
  36.7 4.7 collective-permute-start.7
  75.9 9.6 %collective-permute-done.8 = bf16[272,384]{1,0:T(8,128)(2,1)} collective-permute-done((bf16[272,384]{1,0:T(8,128)(2,1)}, bf16[272,384]{1,0:T(8,128)(2,1)}, u32[]{:S(2)}, u32[]{:S(2)}) %collective-permute-start.8) | collective-permute-done | bytes 208928 | tf_op jit(solution)/shard_map/ppermute | solution.py:67
  102.2 15.1 %collective-permute-done.11 = bf16[272,384]{1,0:T(8,128)(2,1)S(1)} collective-permute-done((bf16[272,384]{1,0:T(8,128)(2,1)}, bf16[272,384]{1,0:T(8,128)(2,1)S(1)}, u32[]{:S(2)}, u32[]{:S(2)}) %collective-permute-start.11) | collective-permute-done | bytes 208928 | tf_op jit(solution)/shard_map/ppermute | solution.py:63
  119.9 4.5 dynamic_update_slice.49
  140.6 5.4 collective-permute-done.19
  156.9 7.6 %collective-permute-done.22 = bf16[272,960]{1,0:T(8,128)(2,1)S(1)} collective-permute-done((bf16[272,960]{1,0:T(8,128)(2,1)S(1)}, bf16[272,960]{1,0:T(8,128)(2,1)S(1)}, u32[]{:S(2)}, u32[]{:S(2)}) %collective-permute-start.22) | collective-permute-done | bytes 522272 | tf_op jit(solution)/shard_map/ppermute | solution.py:63
  182.4 12.2 %collective-permute-done.31 = bf16[272,1088]{1,0:T(8,128)(2,1)S(1)} collective-permute-done((bf16[272,1088]{1,0:T(8,128)(2,1)}, bf16[272,1088]{1,0:T(8,128)(2,1)S(1)}, u32[]{:S(2)}, u32[]{:S(2)}) %collective-permute-start.31) | collective-permute-done | bytes 591904 | tf_op jit(solution)/shard_map/ppermute | solution.py:63
  198.8 11.2 %collective-permute-done.32 = bf16[272,1088]{1,0:T(8,128)(2,1)S(1)} collective-permute-done((bf16[272,1088]{1,0:T(8,128)(2,1)S(1)}, bf16[272,1088]{1,0:T(8,128)(2,1)S(1)}, u32[]{:S(2)}, u32[]{:S(2)}) %collective-permute-start.32) | collective-permute-done | bytes 591904 | tf_op jit(solution)/shard_map/ppermute | solution.py:63
  227.6 12.2 %collective-permute-done.77 = bf16[272,1088]{1,0:T(8,128)(2,1)} collective-permute-done((bf16[272,1088]{1,0:T(8,128)(2,1)}, bf16[272,1088]{1,0:T(8,128)(2,1)}, u32[]{:S(2)}, u32[]{:S(2)}) %collective-permute-start.77) | collective-permute-done | bytes 591904 | tf_op jit(solution)/shard_map/ppermute | solution.py:67
  239.8 9.5 %collective-permute-done.75 = bf16[272,1088]{1,0:T(8,128)(2,1)} collective-permute-done((bf16[272,1088]{1,0:T(8,128)(2,1)}, bf16[272,1088]{1,0:T(8,128)(2,1)}, u32[]{:S(2)}, u32[]{:S(2)}) %collective-permute-start.75) | collective-permute-done | bytes 591904 | tf_op jit(solution)/shard_map/ppermute | solution.py:63
  258.9 10.6 %collective-permute-done.78 = bf16[272,1088]{1,0:T(8,128)(2,1)} collective-permute-done((bf16[272,1088]{1,0:T(8,128)(2,1)}, bf16[272,1088]{1,0:T(8,128)(2,1)}, u32[]{:S(2)}, u32[]{:S(2)}) %collective-permute-start.78) | collective-permute-done | bytes 591904 | tf_op jit(solution)/shard_map/ppermute | solution.py:67
  275.1 13.1 %collective-permute-done.79 = bf16[272,1088]{1,0:T(8,128)(2,1)} collective-permute-done((bf16[272,1088]{1,0:T(8,128)(2,1)}, bf16[272,1088]{1,0:T(8,128)(2,1)}, u32[]{:S(2)}, u32[]{:S(2)}) %collective-permute-start.79) | collective-permute-done | bytes 591904 | tf_op jit(solution)/shard_map/ppermute | solution.py:67
  293.0 5.7 collective-permute-done.80
  303.6 5.4 collective-permute-done.33
  319.2 5.8 collective-permute-done.35
  325.0 5.0 collective-permute-start.36
  356.7 8.2 %collective-permute-done.38 = bf16[272,1088]{1,0:T(8,128)(2,1)S(1)} collective-permute-done((bf16[272,1088]{1,0:T(8,128)(2,1)}, bf16[272,1088]{1,0:T(8,128)(2,1)S(1)}, u32[]{:S(2)}, u32[]{:S(2)}) %collective-permute-start.38) | collective-permute-done | bytes 591904 | tf_op jit(solution)/shard_map/ppermute | solution.py:63
  372.3 4.6 collective-permute-done.39
  379.1 5.5 fusion.118
  394.9 14.9 %collective-permute-done.70 = bf16[288,1088]{1,0:T(8,128)(2,1)S(1)} collective-permute-done((bf16[288,1088]{1,0:T(8,128)(2,1)S(1)}, bf16[288,1088]{1,0:T(8,128)(2,1)S(1)}, u32[]{:S(2)}, u32[]{:S(2)}) %collective-permute-start.70) | collective-permute-done | bytes 626720 | tf_op jit(solution)/shard_map/ppermute | solution.py:67
  412.7 4.6 collective-permute-start.71
  417.3 4.5 convolution_convert_fusion.4
  423.2 6.9 %collective-permute-done.68 = bf16[288,1088]{1,0:T(8,128)(2,1)} collective-permute-done((bf16[288,1088]{1,0:T(8,128)(2,1)}, bf16[288,1088]{1,0:T(8,128)(2,1)}, u32[]{:S(2)}, u32[]{:S(2)}) %collective-permute-start.68) | collective-permute-done | bytes 626720 | tf_op jit(solution)/shard_map/ppermute | solution.py:63
  436.7 4.4 collective-permute-start.72
  480.7 4.9 collective-permute-start.64
  489.6 5.3 collective-permute-start.62
  522.1 4.6 collective-permute-start.57
  532.9 6.1 collective-permute-done.54
  556.1 6.1 collective-permute-done.82
  572.0 5.2 collective-permute-start.83
  579.5 5.6 collective-permute-done.83
  591.3 5.6 collective-permute-done.59
  (602 shorter events, 350.6 us)
Async XLA Ops:
  7.2 502.2 %reduce-scatter.2.cloned.1.call-start = ((), (), s32[]{:S(2)}) async-start(), calls=%async_computation.1 | async-start | bytes 1392640 | tf_op jit(solution)/shard_map/reduce_scatter | solution.py:326
  10.3 36.6 %collective-permute-start.12 = (bf16[288,408]{1,0:T(8,128)(2,1)}, bf16[288,408]{1,0:T(8,128)(2,1)}, u32[]{:S(2)}, u32[]{:S(2)}) collective-permute-start(bf16[288,408]{1,0:T(8,128)(2,1)} %pad_maximum_fusion.30), channel_id=1, source_target_pairs={{0,16},{16,0},{1,17},{17,1},{2,18},{18,2},{3,19},{19,3},{4,20},{20... | collective-permute-start | bytes 705032 | tf_op jit(solution)/shard_map/ppermute | solution.py:152
  11.8 47.0 %collective-permute-start = (bf16[512,272]{0,1:T(8,128)(2,1)}, bf16[512,272]{0,1:T(8,128)(2,1)S(1)}, u32[]{:S(2)}, u32[]{:S(2)}) collective-permute-start(bf16[512,272]{0,1:T(8,128)(2,1)} %param.23), channel_id=1, source_target_pairs={{0,0},{1,4},{2,8},{3,12},{4,1},{5,5},{6,9},{7,13},{8,2},{9,6},{10,... | collective-permute-start | bytes 835592 | tf_op jit(solution)/shard_map/ppermute | solution.py:45
  20.3 28.3 %collective-permute-start.26 = (bf16[288,544]{1,0:T(8,128)(2,1)}, bf16[288,544]{1,0:T(8,128)(2,1)}, u32[]{:S(2)}, u32[]{:S(2)}) collective-permute-start(bf16[288,544]{1,0:T(8,128)(2,1)} %pad_maximum_fusion.28), channel_id=1, source_target_pairs={{0,16},{16,0},{1,17},{17,1},{2,18},{18,2},{3,19},{19,3},{4,20},{20... | collective-permute-start | bytes 940040 | tf_op jit(solution)/shard_map/ppermute | solution.py:152
  29.2 34.4 %collective-permute-start.41 = (bf16[512,272]{0,1:T(8,128)(2,1)}, bf16[512,272]{0,1:T(8,128)(2,1)S(1)}, u32[]{:S(2)}, u32[]{:S(2)}) collective-permute-start(bf16[512,272]{0,1:T(8,128)(2,1)} %param.24), channel_id=1, source_target_pairs={{0,0},{1,4},{2,8},{3,12},{4,1},{5,5},{6,9},{7,13},{8,2},{9,6},{10,... | collective-permute-start | bytes 835592 | tf_op jit(solution)/shard_map/ppermute | solution.py:45
  36.7 26.9 %collective-permute-start.7 = (bf16[272,384]{1,0:T(8,128)(2,1)}, bf16[272,384]{1,0:T(8,128)(2,1)}, u32[]{:S(2)}, u32[]{:S(2)}) collective-permute-start(bf16[272,384]{1,0:T(8,128)(2,1)} %maximum_select_fusion.6), channel_id=1, source_target_pairs={{4,0},{8,4},{12,8},{5,1},{9,5},{13,9},{6,2},{10,6},{14,10},{7,3},{... | collective-permute-start | bytes 626696 | tf_op jit(solution)/shard_map/ppermute | solution.py:67
  63.6 29.4 %collective-permute-start.1 = (bf16[512,272]{0,1:T(8,128)(2,1)S(1)}, bf16[512,272]{0,1:T(8,128)(2,1)}, u32[]{:S(2)}, u32[]{:S(2)}) collective-permute-start(bf16[512,272]{0,1:T(8,128)(2,1)S(1)} %collective-permute-done), channel_id=1, source_target_pairs={{0,1},{1,0},{2,3},{3,2},{4,5},{5,4},{6,7},{7,6},{8,9},{9,8},{10,11... | collective-permute-start | bytes 835592 | tf_op jit(solution)/shard_map/ppermute | solution.py:115
  63.6 31.9 %collective-permute-start.42 = (bf16[512,272]{0,1:T(8,128)(2,1)S(1)}, bf16[512,272]{0,1:T(8,128)(2,1)}, u32[]{:S(2)}, u32[]{:S(2)}) collective-permute-start(bf16[512,272]{0,1:T(8,128)(2,1)S(1)} %collective-permute-done.41), channel_id=1, source_target_pairs={{0,1},{1,0},{2,3},{3,2},{4,5},{5,4},{6,7},{7,6},{8,9},{9,8},{10,11... | collective-permute-start | bytes 835592 | tf_op jit(solution)/shard_map/ppermute | solution.py:115
  64.1 69.2 %collective-permute-start.28 = (bf16[272,1088]{1,0:T(8,128)(2,1)}, bf16[272,1088]{1,0:T(8,128)(2,1)}, u32[]{:S(2)}, u32[]{:S(2)}) collective-permute-start(bf16[272,1088]{1,0:T(8,128)(2,1)} %get-tuple-element.229), channel_id=1, source_target_pairs={{4,0},{8,4},{12,8},{5,1},{9,5},{13,9},{6,2},{10,6},{14,10},{7,3},{... | collective-permute-start | bytes 1775624 | tf_op jit(solution)/shard_map/ppermute | solution.py:67
  85.5 89.1 %collective-permute-start.27 = (bf16[272,1088]{1,0:T(8,128)(2,1)}, bf16[272,1088]{1,0:T(8,128)(2,1)}, u32[]{:S(2)}, u32[]{:S(2)}) collective-permute-start(bf16[272,1088]{1,0:T(8,128)(2,1)} %get-tuple-element.229), channel_id=1, source_target_pairs={{0,4},{4,8},{8,12},{1,5},{5,9},{9,13},{2,6},{6,10},{10,14},{3,7},{... | collective-permute-start | bytes 1775624 | tf_op jit(solution)/shard_map/ppermute | solution.py:63
  87.5 43.9 %collective-permute-start.18 = (bf16[272,960]{1,0:T(8,128)(2,1)}, bf16[272,960]{1,0:T(8,128)(2,1)}, u32[]{:S(2)}, u32[]{:S(2)}) collective-permute-start(bf16[272,960]{1,0:T(8,128)(2,1)} %get-tuple-element.168), channel_id=1, source_target_pairs={{4,0},{8,4},{12,8},{5,1},{9,5},{13,9},{6,2},{10,6},{14,10},{7,3},{... | collective-permute-start | bytes 1566728 | tf_op jit(solution)/shard_map/ppermute | solution.py:67
  95.6 39.1 %collective-permute-start.17 = (bf16[272,960]{1,0:T(8,128)(2,1)}, bf16[272,960]{1,0:T(8,128)(2,1)}, u32[]{:S(2)}, u32[]{:S(2)}) collective-permute-start(bf16[272,960]{1,0:T(8,128)(2,1)} %get-tuple-element.168), channel_id=1, source_target_pairs={{0,4},{4,8},{8,12},{1,5},{5,9},{9,13},{2,6},{6,10},{10,14},{3,7},{... | collective-permute-start | bytes 1566728 | tf_op jit(solution)/shard_map/ppermute | solution.py:63
  133.4 44.8 %collective-permute-start.43 = (bf16[2,512,272]{1,2,0:T(8,128)(2,1)}, bf16[2,512,272]{1,2,0:T(8,128)(2,1)}, u32[]{:S(2)}, u32[]{:S(2)}) collective-permute-start(bf16[2,512,272]{1,2,0:T(8,128)(2,1)} %pad_maximum_fusion.26), channel_id=1, source_target_pairs={{0,2},{1,3},{2,0},{3,1},{4,6},{5,7},{6,4},{7,5},{8,10},{9,11},{10,... | collective-permute-start | bytes 1671176 | tf_op jit(solution)/shard_map/ppermute | solution.py:115
  134.7 44.7 %collective-permute-start.29 = (bf16[272,1088]{1,0:T(8,128)(2,1)}, bf16[272,1088]{1,0:T(8,128)(2,1)}, u32[]{:S(2)}, u32[]{:S(2)}) collective-permute-start(bf16[272,1088]{1,0:T(8,128)(2,1)} %collective-permute-done.28), channel_id=1, source_target_pairs={{4,0},{8,4},{5,1},{9,5},{6,2},{10,6},{7,3},{11,7},{20,16},{24,20},... | collective-permute-start | bytes 1775624 | tf_op jit(solution)/shard_map/ppermute | solution.py:67
  174.7 19.9 %collective-permute-start.31 = (bf16[272,1088]{1,0:T(8,128)(2,1)}, bf16[272,1088]{1,0:T(8,128)(2,1)S(1)}, u32[]{:S(2)}, u32[]{:S(2)}) collective-permute-start(bf16[272,1088]{1,0:T(8,128)(2,1)} %collective-permute-done.27), channel_id=1, source_target_pairs={{4,8},{8,12},{5,9},{9,13},{6,10},{10,14},{7,11},{11,15},{20,24},{2... | collective-permute-start | bytes 1775624 | tf_op jit(solution)/shard_map/ppermute | solution.py:63
  226.3 23.0 %collective-permute-start.75 = (bf16[272,1088]{1,0:T(8,128)(2,1)}, bf16[272,1088]{1,0:T(8,128)(2,1)}, u32[]{:S(2)}, u32[]{:S(2)}) collective-permute-start(bf16[272,1088]{1,0:T(8,128)(2,1)} %add_convert_fusion.12), channel_id=1, source_target_pairs={{0,4},{4,8},{1,5},{5,9},{2,6},{6,10},{3,7},{7,11},{16,20},{20,24},... | collective-permute-start | bytes 1775624 | tf_op jit(solution)/shard_map/ppermute | solution.py:63
  255.9 19.3 %collective-permute-start.76 = (bf16[272,1088]{1,0:T(8,128)(2,1)}, bf16[272,1088]{1,0:T(8,128)(2,1)}, u32[]{:S(2)}, u32[]{:S(2)}) collective-permute-start(bf16[272,1088]{1,0:T(8,128)(2,1)} %get-tuple-element.171), channel_id=1, source_target_pairs={{0,4},{4,8},{8,12},{1,5},{5,9},{9,13},{2,6},{6,10},{10,14},{3,7},{... | collective-permute-start | bytes 1775624 | tf_op jit(solution)/shard_map/ppermute | solution.py:63
  315.6 35.0 %collective-permute-start.34 = (bf16[272,1088]{1,0:T(8,128)(2,1)}, bf16[272,1088]{1,0:T(8,128)(2,1)}, u32[]{:S(2)}, u32[]{:S(2)}) collective-permute-start(bf16[272,1088]{1,0:T(8,128)(2,1)} %get-tuple-element.170), channel_id=1, source_target_pairs={{0,4},{4,8},{8,12},{1,5},{5,9},{9,13},{2,6},{6,10},{10,14},{3,7},{... | collective-permute-start | bytes 1775624 | tf_op jit(solution)/shard_map/ppermute | solution.py:63
  325.0 27.5 %collective-permute-start.36 = (bf16[272,1088]{1,0:T(8,128)(2,1)}, bf16[272,1088]{1,0:T(8,128)(2,1)}, u32[]{:S(2)}, u32[]{:S(2)}) collective-permute-start(bf16[272,1088]{1,0:T(8,128)(2,1)} %collective-permute-done.35), channel_id=1, source_target_pairs={{4,0},{8,4},{5,1},{9,5},{6,2},{10,6},{7,3},{11,7},{20,16},{24,20},... | collective-permute-start | bytes 1775624 | tf_op jit(solution)/shard_map/ppermute | solution.py:67
  394.1 27.7 %collective-permute-start.45 = (bf16[256,1088]{0,1:T(8,128)(2,1)}, bf16[256,1088]{0,1:T(8,128)(2,1)}, u32[]{:S(2)}, u32[]{:S(2)}) collective-permute-start(bf16[256,1088]{0,1:T(8,128)(2,1)} %add_convert_fusion.16), channel_id=1, source_target_pairs={{0,2},{1,3},{2,0},{3,1},{4,6},{5,7},{6,4},{7,5},{8,10},{9,11},{10,... | collective-permute-start | bytes 1671176 | tf_op jit(solution)/shard_map/ppermute | solution.py:115
  434.6 33.2 %collective-permute-start.69 = (bf16[288,1088]{1,0:T(8,128)(2,1)}, bf16[288,1088]{1,0:T(8,128)(2,1)}, u32[]{:S(2)}, u32[]{:S(2)}) collective-permute-start(bf16[288,1088]{1,0:T(8,128)(2,1)} %get-tuple-element.250), channel_id=1, source_target_pairs={{0,4},{4,8},{8,12},{1,5},{5,9},{9,13},{2,6},{6,10},{10,14},{3,7},{... | collective-permute-start | bytes 1880072 | tf_op jit(solution)/shard_map/ppermute | solution.py:63
  436.7 32.4 %collective-permute-start.72 = (bf16[288,1088]{1,0:T(8,128)(2,1)}, bf16[288,1088]{1,0:T(8,128)(2,1)}, u32[]{:S(2)}, u32[]{:S(2)}) collective-permute-start(bf16[288,1088]{1,0:T(8,128)(2,1)} %get-tuple-element.251), channel_id=1, source_target_pairs={{4,0},{8,4},{12,8},{5,1},{9,5},{13,9},{6,2},{10,6},{14,10},{7,3},{... | collective-permute-start | bytes 1880072 | tf_op jit(solution)/shard_map/ppermute | solution.py:67
  455.6 49.5 %collective-permute-start.47 = (bf16[256,1088]{0,1:T(8,128)(2,1)}, bf16[256,1088]{0,1:T(8,128)(2,1)}, u32[]{:S(2)}, u32[]{:S(2)}) collective-permute-start(bf16[256,1088]{0,1:T(8,128)(2,1)} %constant_dynamic-slice_fusion.29), channel_id=1, source_target_pairs={{0,1},{1,0},{2,3},{3,2},{4,5},{5,4},{6,7},{7,6},{8,9},{9,8},{10,11... | collective-permute-start | bytes 1671176 | tf_op jit(solution)/shard_map/ppermute | solution.py:115
  474.6 20.5 %collective-permute-start.73 = (bf16[288,544]{1,0:T(8,128)(2,1)S(1)}, bf16[288,544]{1,0:T(8,128)(2,1)S(1)}, u32[]{:S(2)}, u32[]{:S(2)}) collective-permute-start(bf16[288,544]{1,0:T(8,128)(2,1)S(1)} %constant_dynamic-slice_fusion.12), channel_id=1, source_target_pairs={{0,16},{16,0},{1,17},{17,1},{2,18},{18,2},{3,19},{19,3},{4,20},{20... | collective-permute-start | bytes 940040 | tf_op jit(solution)/shard_map/ppermute | solution.py:188
  486.8 31.5 %collective-permute-start.53 = (bf16[288,816]{1,0:T(8,128)(2,1)}, bf16[288,816]{1,0:T(8,128)(2,1)}, u32[]{:S(2)}, u32[]{:S(2)}) collective-permute-start(bf16[288,816]{1,0:T(8,128)(2,1)} %get-tuple-element.260), channel_id=1, source_target_pairs={{0,4},{1,5},{2,6},{3,7},{16,20},{17,21},{18,22},{19,23}} | collective-permute-start | bytes 1410056 | tf_op jit(solution)/shard_map/ppermute | solution.py:63
  488.3 30.0 %collective-permute-start.56 = (bf16[288,816]{1,0:T(8,128)(2,1)}, bf16[288,816]{1,0:T(8,128)(2,1)}, u32[]{:S(2)}, u32[]{:S(2)}) collective-permute-start(bf16[288,816]{1,0:T(8,128)(2,1)} %get-tuple-element.261), channel_id=1, source_target_pairs={{12,8},{13,9},{14,10},{15,11},{28,24},{29,25},{30,26},{31,27}} | collective-permute-start | bytes 1410056 | tf_op jit(solution)/shard_map/ppermute | solution.py:67
  507.1 19.6 %collective-permute-start.48 = (bf16[256,1088]{0,1:T(8,128)(2,1)}, bf16[256,1088]{0,1:T(8,128)(2,1)}, u32[]{:S(2)}, u32[]{:S(2)}) collective-permute-start(bf16[256,1088]{0,1:T(8,128)(2,1)} %add_convert_fusion.14), channel_id=1, source_target_pairs={{0,2},{1,3},{2,0},{3,1},{4,6},{5,7},{6,4},{7,5},{8,10},{9,11},{10,... | collective-permute-start | bytes 1671176 | tf_op jit(solution)/shard_map/ppermute | solution.py:115
  511.3 21.5 %collective-permute-start.40 = (bf16[512,272]{0,1:T(8,128)(2,1)}, bf16[512,272]{0,1:T(8,128)(2,1)}, u32[]{:S(2)}, u32[]{:S(2)}) collective-permute-start(bf16[512,272]{0,1:T(8,128)(2,1)} %add_convert_fusion.24), channel_id=1, source_target_pairs={{0,0},{1,4},{2,8},{3,12},{4,1},{5,5},{6,9},{7,13},{8,2},{9,6},{10,... | collective-permute-start | bytes 835592 | tf_op jit(solution)/shard_map/ppermute | solution.py:45
  528.1 19.8 %collective-permute-start.49 = (bf16[256,1088]{0,1:T(8,128)(2,1)S(1)}, bf16[256,1088]{0,1:T(8,128)(2,1)S(1)}, u32[]{:S(2)}, u32[]{:S(2)}) collective-permute-start(bf16[256,1088]{0,1:T(8,128)(2,1)S(1)} %add_convert_fusion.13), channel_id=1, source_target_pairs={{0,1},{1,0},{2,3},{3,2},{4,5},{5,4},{6,7},{7,6},{8,9},{9,8},{10,11... | collective-permute-start | bytes 1671176 | tf_op jit(solution)/shard_map/ppermute | solution.py:115
  541.7 37.5 %collective-permute-start.55 = (bf16[288,816]{1,0:T(8,128)(2,1)}, bf16[288,816]{1,0:T(8,128)(2,1)S(1)}, u32[]{:S(2)}, u32[]{:S(2)}) collective-permute-start(bf16[288,816]{1,0:T(8,128)(2,1)} %get-tuple-element.256), channel_id=1, source_target_pairs={{0,4},{4,8},{8,12},{1,5},{5,9},{9,13},{2,6},{6,10},{10,14},{3,7},{... | collective-permute-start | bytes 1410056 | tf_op jit(solution)/shard_map/ppermute | solution.py:63
  543.6 35.6 %collective-permute-start.58 = (bf16[288,816]{1,0:T(8,128)(2,1)}, bf16[288,816]{1,0:T(8,128)(2,1)S(1)}, u32[]{:S(2)}, u32[]{:S(2)}) collective-permute-start(bf16[288,816]{1,0:T(8,128)(2,1)} %get-tuple-element.257), channel_id=1, source_target_pairs={{4,0},{8,4},{12,8},{5,1},{9,5},{13,9},{6,2},{10,6},{14,10},{7,3},{... | collective-permute-start | bytes 1410056 | tf_op jit(solution)/shard_map/ppermute | solution.py:67
  571.2 33.1 %collective-permute-start.50 = (bf16[512,272]{0,1:T(8,128)(2,1)S(1)}, bf16[512,272]{0,1:T(8,128)(2,1)S(1)}, u32[]{:S(2)}, u32[]{:S(2)}) collective-permute-start(bf16[512,272]{0,1:T(8,128)(2,1)S(1)} %fusion.45), channel_id=1, source_target_pairs={{0,0},{1,4},{2,8},{3,12},{4,1},{5,5},{6,9},{7,13},{8,2},{9,6},{10,... | collective-permute-start | bytes 835592 | tf_op jit(solution)/shard_map/ppermute | solution.py:45
  (175 other events, 2361.0 us)
Sparse Core Ops, SparseCore 0:
  421.9 24.4 reduce-scatter.1
